TPU v7x, 512 devices: a whole 4x8x8 slice. The times are simulated.
512 devices in a mesh: tm: 32 (over z_lo, y, core), space: 16 (over z_hi, x).
Axes of the slice: x: 4, y: 8, z: 8 (z_hi: 4, z_lo: 2; z = z_hi * 2 + z_lo), core: 2. Of those that a mesh axis runs over, the one named last changes fastest.
Arguments:
- starts: float32 [32, 256, 128, 128], P('tm', 'space'), may hold values from -6 to 6
- holes: int32 [256, 128, 128], P('space'), may hold values 0 or 1
- rate: float32 [256, 128, 128], P('space'), may hold values from 0.05 to 50
- zones: int32 [2, 256, 128], P(None, 'space'), may hold values from 0 to 7
- zone_htc: float32 [8], replicated, may hold values from 0.3 to 4
- gas: float32 [32, 8], P('tm'), may hold values from -1 to 2
- hold: float32 [32], P('tm'), may hold values from 0.5 to 1
- duration: float32 [32], P('tm'), may hold values from 0.5 to 1.5
- inv_x: bfloat16 [128, 128], replicated, may hold values from 0 to 1, as said below
- inv_y: bfloat16 [128, 128], replicated, may hold values from 0 to 1, as said below
- inv_z: bfloat16 [256, 256], replicated, may hold values from 0 to 1, as said below
Outputs:
- renewed_starts: float32 [32, 256, 128, 128], P('tm', 'space')
Inputs may be any that keep to these rules, and one draw needn't show every extreme that they name: `inv_x`: entries are positive. `inv_y`: entries are positive. `inv_z`: entries are positive.
All inputs are finite; a program needn't handle non-finite values. No bound on the sum of `holes` on one device may be relied on, other than what follows from the above.
Results may differ from a plain program's by a relative error of at most 0.0003.
Values may be sent and summed in bfloat16 or wider, within the bound.
A program may use at most 128 MiB of HBM per device.

v0:
```python
import jax
import jax.numpy as jnp
from jax import lax
from jax.sharding import PartitionSpec as P

COOLING = 4.0
COOLANT = -1.0
TIME_STEP = 0.2


def padded_2(shard, sides, width):
    for axis, dim in sides:
        peers, length = (lax.axis_size(axis), shard.shape[dim])
        up = [(i, (i + 1) % peers) for i in range(peers - 1)]
        down = [(j, i) for i, j in up]
        last = lax.slice_in_dim(shard, length - width, length, axis=dim)
        leading = lax.slice_in_dim(shard, 0, width, axis=dim)
        before = lax.ppermute(last, axis, up)
        after = lax.ppermute(leading, axis, down)
        shard = jnp.concatenate([before, shard, after], axis=dim)
    return shard


def entering(part, axis, combine, identity):
    place = lax.axis_index(axis)
    gathered = jax.tree.map(lambda a: lax.all_gather(a, axis), part)
    state = jax.tree.map(lambda a, e: jnp.zeros_like(a) + jnp.asarray(e, a.dtype), part, identity)

    def one(hop, state):
        return combine(
            state, jax.tree.map(lambda a: lax.dynamic_index_in_dim(a, hop, 0, False), gathered)
        )

    return lax.fori_loop(0, place, one, state)


def spread(block, axis, source):
    block = jnp.where(lax.axis_index(axis) == source, block, jnp.zeros_like(block))
    return lax.psum(block, axis)


def passed_along(block, axis, distance):
    devices = range(lax.axis_size(axis))
    route = [((i - distance) % len(devices), i) for i in devices]
    return lax.ppermute(block, axis, route)


def conduct(values):
    return 1.0 + 0.5 * jnp.tanh(values)


def face_tables(zones, zone_htc, gas_row):
    onehot = (zones[..., None] == jnp.arange(zone_htc.shape[0], dtype=jnp.int32)).astype(
        zone_htc.dtype
    )
    return (jnp.sum(onehot * zone_htc, axis=-1), jnp.sum(onehot * gas_row, axis=-1))


def step_increment(zpadded, holes, face_coef, face_temp):
    padded = jnp.pad(zpadded, ((0, 0), (1, 1), (1, 1)))
    conducts = conduct(padded)
    centre = padded[1:-1, 1:-1, 1:-1]
    centre_k = conducts[1:-1, 1:-1, 1:-1]
    neighbours = [
        (padded[2:, 1:-1, 1:-1], conducts[2:, 1:-1, 1:-1]),
        (padded[:-2, 1:-1, 1:-1], conducts[:-2, 1:-1, 1:-1]),
        (padded[1:-1, 2:, 1:-1], conducts[1:-1, 2:, 1:-1]),
        (padded[1:-1, :-2, 1:-1], conducts[1:-1, :-2, 1:-1]),
        (padded[1:-1, 1:-1, 2:], conducts[1:-1, 1:-1, 2:]),
        (padded[1:-1, 1:-1, :-2], conducts[1:-1, 1:-1, :-2]),
    ]
    flux = jnp.zeros_like(centre)
    for neighbour, neighbour_k in neighbours:
        flux = flux + 0.5 * (centre_k + neighbour_k) * (neighbour - centre)
    column = lax.broadcasted_iota(jnp.int32, centre.shape, 2)
    first_face = jnp.where(
        column == 0, face_coef[0][:, :, None] * (face_temp[0][:, :, None] - centre), 0.0
    )
    last_face = jnp.where(
        column == centre.shape[2] - 1,
        face_coef[1][:, :, None] * (face_temp[1][:, :, None] - centre),
        0.0,
    )
    surface = first_face + last_face
    cooled = COOLING * holes.astype(centre.dtype) * (COOLANT - centre)
    return (TIME_STEP * (flux + surface + cooled)).astype(jnp.bfloat16)


def across_x(inverse, values):
    return jnp.einsum("ab,zby->zay", inverse, values, preferred_element_type=jnp.float32)


def across_y(inverse, values):
    return jnp.einsum("zxb,ab->zxa", values, inverse, preferred_element_type=jnp.float32)


def across_z(inverse, values):
    return jnp.einsum("ab,bxy->axy", inverse, values, preferred_element_type=jnp.float32)


def plane_steps(zpadded, holes, face_coef, face_temp, inv_x, inv_y):
    increment = step_increment(zpadded, holes, face_coef, face_temp)
    return across_y(inv_y, across_x(inv_x, increment).astype(jnp.bfloat16))


def widened(field):
    return padded_2(field, (("space", 0),), 1)


def per_device(starts, holes, rate, zones, zone_htc, gas, hold, duration, inv_x, inv_y, inv_z):
    windows = lax.axis_size("tm")
    current = starts[0]
    holding = hold[0]
    length = duration[0]
    face_coef, face_temp = face_tables(zones, zone_htc, gas[0])
    factor = holding * jnp.exp(-rate * length / windows)

    def compose(earlier, later):
        first_len, first_hold, first_sum = earlier
        second_len, second_hold, second_sum = later
        propagated_state = second_hold * jnp.exp(-rate * second_len / windows) * first_sum
        return (first_len + second_len, first_hold * second_hold, propagated_state + second_sum)

    unit_matrix = (jnp.zeros((), jnp.float32), jnp.ones((), jnp.float32), jnp.zeros_like(current))
    planar = plane_steps(widened(current), holes, face_coef, face_temp, inv_x, inv_y)
    vertical_lines = across_z(
        inv_z,
        lax.all_to_all(
            planar.astype(jnp.bfloat16), "space", split_axis=1, concat_axis=0, tiled=True
        ),
    )
    vertical = lax.all_to_all(vertical_lines, "space", split_axis=0, concat_axis=1, tiled=True)
    defect = vertical - planar
    affine_update = current + vertical - factor * current
    own = (length, holding, affine_update)
    before = entering(own, "tm", compose, unit_matrix)
    running_totals = compose(before, own)
    length_all = spread(running_totals[0], "tm", windows - 1)
    hold_everything = spread(running_totals[1], "tm", windows - 1)
    total = spread(running_totals[2], "tm", windows - 1)
    anchor = total / (1.0 - hold_everything * jnp.exp(-rate * length_all / windows))
    predicted = before[1] * jnp.exp(-rate * before[0] / windows) * anchor + before[2]
    coarse = plane_steps(widened(predicted), holes, face_coef, face_temp, inv_x, inv_y)
    renewed = predicted + coarse + defect
    current = passed_along(renewed, "tm", 1)
    return current[None]


def solution(mesh):
    return jax.shard_map(
        per_device,
        mesh=mesh,
        in_specs=(
            P("tm", "space", None, None),
            P("space", None, None),
            P("space", None, None),
            P(None, "space", None),
            P(),
            P("tm", None),
            P("tm"),
            P("tm"),
            P(),
            P(),
            P(),
        ),
        out_specs=P("tm", "space", None, None),
        check_vma=False,
    )
```

profile of v0, /device:TPU:134, one launch (start us, length us, event | category | flops | bytes accessed | tf_op | source)
XLA Modules:
  0.0 751.9 jit_solution(9392594457783241285)
XLA Ops:
  7.5 7.2 collective-permute-start
  14.7 1.9 collective-permute-start.1
  17.5 8.2 %collective-permute-done.1 = f32[1,128,128]{2,1,0:T(8,128)S(1)} collective-permute-done((f32[1,128,128]{2,1,0:T(8,128)S(1)}, f32[1,128,128]{2,1,0:T(8,128)S(1)}, u32[]{:S(2)}, u32[]{:S(2)}) %collective-permute-start.1) | collective-permute-done | bytes 65568 | tf_op jit(solution)/shard_map/ppermute | solution.py:19
  25.7 4.4 multiply_add_fusion.1
  30.1 13.7 %fusion.159 = (bf16[16,128,128]{2,1,0:T(8,128)(2,1)S(1)}, f32[16,128,128]{2,1,0:T(8,128)}) fusion(bf16[128,128]{1,0:T(8,128)(2,1)S(1)} %copy-done.8, f32[16,128,128]{2,1,0:T(8,128)S(1)} %bitcast.82, f32[18,130,130]{2,1,0:T(8,128)} %get-tuple-element.145, f32[18,130,130]{2,1,0:T(8,128)} %get-tuple-element.144, f32[1,128,128]{2,1,0:T(8,128)S(1)} %collective-permute-done, ...), kind=kOutput, calls=%fused_computation.152 | convolution fusion | flops 146800640 | bytes 15433984 | tf_op jit(solution)/shard_map/zxb,ab->zxa/dot_general | solution.py:94
  44.1 20.0 %all_to_all.36 = bf16[16,128,128]{2,0,1:T(8,128)(2,1)S(1)} all-to-all(bf16[16,128,128]{2,0,1:T(8,128)(2,1)S(1)} %copy.38), channel_id=1, replica_groups=mesh['tm'=32,'space'=16] {'space'}, dimensions={1} | all-to-all | bytes 1048576 | tf_op jit(solution)/shard_map/all_to_all | solution.py:128
  64.7 1.3 copy.42
  66.0 7.1 all-to-all-start.1
  74.4 23.0 %all-to-all-done.1 = f32[256,8,128]{2,1,0:T(8,128)S(1)} async-done(((f32[256,8,128]{2,1,0:T(8,128)}), f32[256,8,128]{2,1,0:T(8,128)S(1)}, u32[]{:S(2)}, u32[]{:S(2)}) %all-to-all-start.1) | async-done | bytes 1048608 | tf_op jit(solution)/shard_map/all_to_all | solution.py:132
  98.4 2.6 fusion.83
  101.0 1.3 dynamic-slice
  103.8 54.9 %all-reduce.5 = (f32[32]{0:T(128)S(1)}, f32[32]{0:T(128)S(1)}) all-reduce(f32[32]{0:T(128)S(1)} %dynamic-update-slice, f32[32]{0:T(128)S(1)} %dynamic-update-slice.1), channel_id=1, replica_groups=mesh['tm'=32,'space'=16] {'tm'}, use_global_device_ids=true, to_apply=%add.2 | all-reduce | flops 64 | bytes 512
  158.7 128.8 %all-gather.3.cloned.1.call-done = f32[512,128,128]{2,1,0:T(8,128)} async-done(((f32[16,128,128]{2,1,0:T(8,128)}), f32[512,128,128]{2,1,0:T(8,128)}) %all-gather.3.cloned.1.call-update) | async-done | bytes 33554448 | tf_op jit(solution)/shard_map/all_gather | solution.py:26
  288.8 2.6 add_select_fusion
  291.5 228.0 %all-reduce.4 = (f32[]{:T(128)}, f32[]{:T(128)}) all-reduce(f32[]{:T(128)S(6)} %select_n.42, f32[]{:T(128)S(6)} %select_n.41), channel_id=1, replica_groups=mesh['tm'=32,'space'=16] {'tm'}, use_global_device_ids=true, to_apply=%region_6.7 | all-reduce | flops 2 | bytes 16 | tf_op jit(solution)/shard_map/psum | solution.py:39
  519.4 169.4 %all-reduce.8.cloned.1.call-done = f32[16,128,128]{2,1,0:T(8,128)} async-done(((f32[16,128,128]{2,1,0:T(8,128)}), f32[16,128,128]{2,1,0:T(8,128)}) %all-reduce.8.cloned.1.call-update) | async-done | bytes 1048592 | tf_op jit(solution)/shard_map/psum | solution.py:39
  688.9 3.0 multiply_add_fusion.2
  691.9 5.5 collective-permute-start.2
  697.4 2.1 collective-permute-start.3
  699.5 9.2 %collective-permute-done.3 = f32[1,128,128]{2,1,0:T(8,128)S(1)} collective-permute-done((f32[1,128,128]{2,1,0:T(8,128)S(1)}, f32[1,128,128]{2,1,0:T(8,128)S(1)}, u32[]{:S(2)}, u32[]{:S(2)}) %collective-permute-start.3) | collective-permute-done | bytes 65568 | tf_op jit(solution)/shard_map/ppermute | solution.py:19
  708.7 3.0 multiply_add_fusion
  711.6 14.0 %fusion.3 = f32[16,128,128]{2,1,0:T(8,128)} fusion(f32[16,128,128]{2,1,0:T(8,128)S(1)} %multiply_add_fusion.2, f32[18,130,130]{2,1,0:T(8,128)} %get-tuple-element.143, f32[18,130,130]{2,1,0:T(8,128)} %get-tuple-element.142, f32[1,128,128]{2,1,0:T(8,128)S(1)} %collective-permute-done.2, f32[1,128,128]{2,1,0:T(8,128)S(1)} %collective-permute-done.3, ...), kind=kOutput, calls=%fused_computation.16 | convolution fusion | flops 147324928 | bytes 18056192 | tf_op jit(solution)/shard_map/zxb,ab->zxa/dot_general | solution.py:94
  725.7 1.9 collective-permute-start.4
  727.6 16.5 %collective-permute-done.4 = f32[16,128,128]{2,1,0:T(8,128)S(1)} collective-permute-done((f32[16,128,128]{2,1,0:T(8,128)}, f32[16,128,128]{2,1,0:T(8,128)S(1)}, u32[]{:S(2)}, u32[]{:S(2)}) %collective-permute-start.4) | collective-permute-done | bytes 1048608 | tf_op jit(solution)/shard_map/ppermute | solution.py:45
  (41 shorter events, 7.5 us)
Async XLA Ops:
  6.5 57.8 %copy-start = (bf16[256,256]{1,0:T(8,128)(2,1)S(1)}, bf16[256,256]{1,0:T(8,128)(2,1)}, u32[]{:S(2)}) copy-start(bf16[256,256]{1,0:T(8,128)(2,1)} %param.23) | copy-start | bytes 393220
  7.5 10.0 %collective-permute-start = (f32[1,128,128]{2,1,0:T(8,128)S(1)}, f32[1,128,128]{2,1,0:T(8,128)S(1)}, u32[]{:S(2)}, u32[]{:S(2)}) collective-permute-start(f32[1,128,128]{2,1,0:T(8,128)S(1)} %get-tuple-element.150), channel_id=1, source_target_pairs={{0,1},{1,2},{2,3},{3,4},{4,5},{5,6},{6,7},{7,8},{8,9},{9,10},{10,1... | collective-permute-start | bytes 196616 | tf_op jit(solution)/shard_map/ppermute | solution.py:18
  14.7 11.0 %collective-permute-start.1 = (f32[1,128,128]{2,1,0:T(8,128)S(1)}, f32[1,128,128]{2,1,0:T(8,128)S(1)}, u32[]{:S(2)}, u32[]{:S(2)}) collective-permute-start(f32[1,128,128]{2,1,0:T(8,128)S(1)} %get-tuple-element.151), channel_id=1, source_target_pairs={{1,0},{2,1},{3,2},{4,3},{5,4},{6,5},{7,6},{8,7},{9,8},{10,9},{11,1... | collective-permute-start | bytes 196616 | tf_op jit(solution)/shard_map/ppermute | solution.py:19
  25.7 4.4 copy-start.4
  25.7 4.4 copy-start.7
  25.7 4.4 copy-start.8
  25.7 4.4 copy-start.9
  64.7 33.7 %copy-start.2 = (f32[16,128,128]{2,1,0:T(8,128)S(1)}, f32[16,128,128]{2,1,0:T(8,128)}, u32[]{:S(2)}) copy-start(f32[16,128,128]{2,1,0:T(8,128)} %param.15) | copy-start | bytes 3145732
  66.0 31.4 %all-to-all-start.1 = ((f32[256,8,128]{2,1,0:T(8,128)}), f32[256,8,128]{2,1,0:T(8,128)S(1)}, u32[]{:S(2)}, u32[]{:S(2)}) async-start(f32[256,8,128]{2,1,0:T(8,128)} %copy.42), calls=%async_computation.1 | async-start | bytes 2097152 | tf_op jit(solution)/shard_map/all_to_all | solution.py:132
  73.1 214.4 %all-gather.3.cloned.1.call-start = ((), (), s32[]{:S(2)}) async-start(), calls=%async_computation.3 | async-start | bytes 34603008 | tf_op jit(solution)/shard_map/all_gather | solution.py:26
  97.4 1.0 copy-start.5
  101.0 587.9 %all-reduce.8.cloned.1.call-start = ((), (), s32[]{:S(2)}) async-start(), calls=%async_computation.2 | async-start | bytes 2097152 | tf_op jit(solution)/shard_map/psum | solution.py:39
  287.6 1.2 copy-start.1
  288.8 400.1 %copy-start.3 = (f32[16,128,128]{2,1,0:T(8,128)S(1)}, f32[16,128,128]{2,1,0:T(8,128)}, u32[]{:S(2)}) copy-start(f32[16,128,128]{2,1,0:T(8,128)} %param.15) | copy-start | bytes 3145732
  691.9 7.6 %collective-permute-start.2 = (f32[1,128,128]{2,1,0:T(8,128)S(1)}, f32[1,128,128]{2,1,0:T(8,128)S(1)}, u32[]{:S(2)}, u32[]{:S(2)}) collective-permute-start(f32[1,128,128]{2,1,0:T(8,128)S(1)} %get-tuple-element.146), channel_id=1, source_target_pairs={{0,1},{1,2},{2,3},{3,4},{4,5},{5,6},{6,7},{7,8},{8,9},{9,10},{10,1... | collective-permute-start | bytes 196616 | tf_op jit(solution)/shard_map/ppermute | solution.py:18
  697.4 14.2 %copy-start.6 = (f32[256,8,128]{2,1,0:T(8,128)S(1)}, f32[256,8,128]{2,1,0:T(8,128)}, u32[]{:S(2)}) copy-start(f32[256,8,128]{2,1,0:T(8,128)} %copy-done.5) | copy-start | bytes 3145732
  697.4 11.2 %collective-permute-start.3 = (f32[1,128,128]{2,1,0:T(8,128)S(1)}, f32[1,128,128]{2,1,0:T(8,128)S(1)}, u32[]{:S(2)}, u32[]{:S(2)}) collective-permute-start(f32[1,128,128]{2,1,0:T(8,128)S(1)} %get-tuple-element.147), channel_id=1, source_target_pairs={{1,0},{2,1},{3,2},{4,3},{5,4},{6,5},{7,6},{8,7},{9,8},{10,9},{11,1... | collective-permute-start | bytes 196616 | tf_op jit(solution)/shard_map/ppermute | solution.py:19
  725.7 18.4 %collective-permute-start.4 = (f32[16,128,128]{2,1,0:T(8,128)}, f32[16,128,128]{2,1,0:T(8,128)S(1)}, u32[]{:S(2)}, u32[]{:S(2)}) collective-permute-start(f32[16,128,128]{2,1,0:T(8,128)} %fusion.3), channel_id=1, source_target_pairs={{496,0},{0,16},{16,32},{32,48},{48,64},{64,80},{80,96},{96,112},{1... | collective-permute-start | bytes 3145736 | tf_op jit(solution)/shard_map/ppermute | solution.py:45
Sparse Core Ops, SparseCore 0:
  101.1 186.3 all-gather.2
  291.6 397.2 all-reduce.7
where the time goes:
time: 755 us; the launch traced here: 752 us
  waiting for transfers between devices  355 us (47%)
  blocking collectives  303 us (40%)
  matrix products  28.1 us (4%)
  starting transfers between devices  25.8 us (3%)
  other arithmetic  16.4 us (2%)
  between operations  14.9 us (2%)
  local copies, waits for them, and re-layouts  8.82 us (1%)
    psum x1, blocking collectives, spread(): return lax.psum(block, axis)  228 us
    psum x1, waiting for transfers between devices, spread(): return lax.psum(block, axis)  169 us
    all_gather x1, waiting for transfers between devices, entering(): gathered = jax.tree.map(lambda a: lax.all_gather(a, axis), part)  129 us
    unnamed x1, blocking collectives  54.9 us
    dot_general x2, matrix products, across_y(): jnp.einsum('zxb,ab->zxa', values, inverse, preferred_element_type=jnp.flo...  27.7 us
    all_to_all x1, waiting for transfers between devices, per_device(): lax.all_to_all(vertical_lines, 'space', split_axis=0, concat_axis=1, tile...  23 us
    all_to_all x1, blocking collectives, per_device(): lax.all_to_all(planar.astype(jnp.bfloat16), 'space', split_axis=1, concat...  20 us
    ppermute x2, waiting for transfers between devices, padded_2(): after = lax.ppermute(leading, axis, down)  17.3 us
  transfers between devices with their start and end apart: 8, of which 6 were waited for; matrix products, arithmetic and copies ran while one was open for 0% of the time, Pallas kernels for 0%

commit v1 on v0

v1 whole, which is shorter than its diff:
```python
import functools

import jax
import jax.numpy as jnp
from jax import lax
from jax.experimental import pallas as pl
from jax.experimental.pallas import tpu as pltpu
from jax.sharding import PartitionSpec as P

COOLING = 4.0
COOLANT = -1.0
TIME_STEP = 0.2
MESH = pl.DeviceIdType.MESH
PIECE = 64
F32 = jnp.float32
BF16 = jnp.bfloat16


def loop(count, body):
    lax.fori_loop(0, count, lambda i, c: (body(i), c)[1], 0)


def kernel(
    T, S,
    u, holes, rate, zones, htc, gas, hold, duration, inv_x, inv_y, inv_z,
    out,
    va, vb, q, iyt, rows_tab, coef_tab, temp_tab, temp_sh, meta, meta_sh, meta_pt,
    u_sh, planar, p_sh, turned, cs, cr, es, er, aff, px, gs, gr, jm, is_, ir, ps,
    halo_s, halo_r, shift_s, shift_r, c_s, c_r, e_s, e_r, pair_s, pair_r,
    g_s, g_r, i_s, i_r, hb_s, hb_r,
):
    t, s = lax.axis_index("tm"), lax.axis_index("space")
    core = lax.rem(t, 2)
    chip = t // 2
    M = T // 2
    mate = t + 1 - 2 * core
    nt, pt = lax.rem(t + 1, T), lax.rem(t + T - 1, T)
    down, up = lax.rem(s + S - 1, S), lax.rem(s + 1, S)
    nz, nx, ny = u.shape
    xb = nx // S
    half = nz * nx // 2
    rb = half // M

    def remote(src, dst, send, recv, tt, ss):
        return pltpu.make_async_remote_copy(
            src_ref=src, dst_ref=dst, send_sem=send, recv_sem=recv,
            device_id=(tt, ss), device_id_type=MESH,
        )

    barrier = pltpu.get_barrier_semaphore()

    def greet(tt, ss):
        pl.semaphore_signal(barrier, inc=1, device_id=(tt, ss), device_id_type=MESH)

    loop(S, lambda k: greet(pt, k))
    loop(S - 1, lambda k: greet(t, lax.rem(s + 1 + k, S)))
    loop(M - 1, lambda k: greet(2 * lax.rem(chip + 1 + k, M) + core, s))
    greet(mate, s)
    greet(mate, lax.rem(s + S - 1 + 2 * core, S))

    number = htc.shape[0]
    zid = zones[...]
    coef = jnp.zeros(zid.shape, F32)
    temp = jnp.zeros(zid.shape, F32)
    for k in range(number):
        coef = jnp.where(zid == k, htc[k], coef)
        temp = jnp.where(zid == k, gas[0, k], temp)
    for tab, values in ((coef_tab, coef), (temp_tab, temp)):
        rows_tab[...] = jnp.zeros_like(rows_tab)
        for z in range(nz):
            rows_tab[2 * z : 2 * z + 1, :] = values[z : z + 1, :]
            at = (2 * z - 1) % ny
            rows_tab[at : at + 1, :] = values[nz + z : nz + z + 1, :]
        tab[...] = rows_tab[...].T
    meta[0:1, :] = jnp.full((1, ny), hold[0], F32)
    meta[1:2, :] = jnp.full((1, ny), duration[0] * (1.0 / T), F32)
    meta[2:8, :] = jnp.zeros((6, ny), F32)
    iyt[...] = inv_y[...].astype(F32).T.astype(BF16)

    pl.semaphore_wait(barrier, S + S - 1 + M - 1 + 2)

    halo = [
        remote(u.at[nz - 1], va.at[0], halo_s.at[0], halo_r.at[0], t, up),
        remote(u.at[0], va.at[nz + 1], halo_s.at[1], halo_r.at[1], t, down),
    ]
    shift = [
        remote(meta, meta_sh, shift_s.at[0], shift_r.at[0], nt, s),
        remote(temp_tab, temp_sh, shift_s.at[1], shift_r.at[1], nt, s),
        remote(u, u_sh, shift_s.at[2], shift_r.at[2], nt, s),
        remote(planar, p_sh, shift_s.at[3], shift_r.at[3], nt, s),
    ]
    for c in halo + shift[:3]:
        c.start()

    row = lax.broadcasted_iota(jnp.int32, (nx, ny), 0)
    lane = lax.broadcasted_iota(jnp.int32, (nx, ny), 1)

    def fill(v, lo, count):
        def one(i):
            z = lo + i
            q[z] = 0.5 + 0.25 * jnp.tanh(v[z])

        loop(count, one)

    def edges(v):
        v[0] = jnp.where(s > 0, v[0], 0.0)
        v[nz + 1] = jnp.where(s < S - 1, v[nz + 1], 0.0)

    def solved(v, z, temps):
        c, qc = v[z + 1], q[z + 1]
        outer = (qc + 0.5) * c
        flux = (q[z + 2] + qc) * (v[z + 2] - c) - (q[z] + qc) * (c - v[z])
        for axis, index, last in ((0, row, nx - 1), (1, lane, ny - 1)):
            n = c.shape[axis]
            vn, qn = pltpu.roll(c, n - 1, axis), pltpu.roll(qc, n - 1, axis)
            ahead = jnp.where(index == last, -outer, (qn + qc) * (vn - c))
            behind = jnp.where(index == 0, outer, pltpu.roll(ahead, 1, axis))
            flux = flux + ahead - behind
        turn = lax.rem(ny - 2 * z, ny)
        face_coef = pltpu.roll(coef_tab[...], turn, 1)
        face_temp = pltpu.roll(temps[...], turn, 1)
        on_face = (lane == 0) | (lane == ny - 1)
        surface = jnp.where(on_face, face_coef * (face_temp - c), 0.0)
        cooled = COOLING * holes[z].astype(F32) * (COOLANT - c)
        e = (TIME_STEP * (flux + surface + cooled)).astype(BF16)
        x = jnp.dot(inv_x[...], e, preferred_element_type=F32).astype(BF16)
        return c, jnp.dot(x, iyt[...], preferred_element_type=F32)

    def own_copy(i):
        va[i + 1] = u[i]

    loop(nz, own_copy)
    fill(va, 1, nz)
    halo[0].wait_recv()
    halo[1].wait_recv()
    edges(va)
    q[0] = 0.5 + 0.25 * jnp.tanh(va[0])
    q[nz + 1] = 0.5 + 0.25 * jnp.tanh(va[nz + 1])

    def first(z):
        _, p = solved(va, z, temp_tab)
        planar[z] = p
        turned[pl.ds(z, nx, stride=nz), :] = p

    loop(nz, first)

    def c_copy(k):
        to = lax.rem(s + 1 + k, S)
        return remote(
            cs.at[pl.ds(to * xb, xb)], cr.at[s], c_s.at[to], c_r.at[s], nt, to
        )

    def c_send(k):
        to = lax.rem(s + 1 + k, S)
        block = turned[pl.ds(to * (xb * nz), xb * nz), :]
        cs[pl.ds(to * xb, xb)] = block.reshape(xb, nz, ny).astype(BF16)
        c_copy(k).start()

    loop(S, c_send)
    shift[3].start()

    shift[0].wait_recv()
    mates = remote(meta_sh, meta_pt, pair_s.at[0], pair_r.at[0], mate, s)
    mates.start()
    shift[2].wait_recv()

    def decay(m, rows):
        return m[0:1, :] * jnp.exp(-(rate[rows, :] * m[1:2, :]))

    def base(i):
        rows = pl.ds(pl.multiple_of(i * nx, nx), nx)
        field = u_sh[i]
        aff[rows, :] = field - decay(meta_sh, rows) * field

    loop(nz, base)

    def c_wait(k):
        remote(cs.at[pl.ds(0, xb)], cr.at[k], c_s.at[k], c_r.at[k], nt, k).wait_recv()

    loop(S, c_wait)
    for x in range(xb):
        lines = cr[:, x].reshape(S * nz, ny)
        es[pl.ds(x, S * nz, stride=xb), :] = jnp.dot(
            inv_z[...], lines, preferred_element_type=F32
        )

    blk = nz * xb

    def e_copy(k):
        to = lax.rem(s + 1 + k, S)
        return remote(es.at[pl.ds(to * blk, blk)], er.at[s], e_s.at[to], e_r.at[s], t, to)

    loop(S - 1, lambda k: e_copy(k).start())
    er[s] = es[pl.ds(s * blk, blk), :]

    def e_wait(k):
        frm = lax.rem(s + 1 + k, S)
        remote(es.at[pl.ds(0, blk)], er.at[frm], e_s.at[frm], e_r.at[frm], t, frm).wait_recv()

    loop(S - 1, e_wait)

    def vertical(z):
        return er[:, pl.ds(pl.multiple_of(z * xb, xb), xb), :].reshape(nx, ny)

    def affine(z):
        rows = pl.ds(pl.multiple_of(z * nx, nx), nx)
        aff[rows, :] = aff[rows, :] + vertical(z)

    loop(nz, affine)
    swap = remote(
        aff.at[pl.ds((1 - core) * half, half)], px, pair_s.at[1], pair_r.at[1], mate, s
    )
    swap.start()
    mates.wait_recv()
    low = jnp.where(core == 0, meta_sh[...], meta_pt[...])
    high = jnp.where(core == 0, meta_pt[...], meta_sh[...])
    both = jnp.concatenate(
        [low[0:1] * high[0:1], low[1:2] + high[1:2], jnp.zeros((6, ny), F32)], axis=0
    )
    swap.wait_recv()

    def place(i):
        return i // (rb // PIECE), lax.rem(i, rb // PIECE) * PIECE

    def pieces(i):
        mine = pl.ds(pl.multiple_of(core * half + i * PIECE, PIECE), PIECE)
        theirs = pl.ds(pl.multiple_of(i * PIECE, PIECE), PIECE)
        own, other = aff[mine, :], px[theirs, :]
        return mine, jnp.where(core == 0, own, other), jnp.where(core == 0, other, own)

    def composed(i):
        block, at = place(i)
        mine, lo, hi = pieces(i)
        gs[block, pl.ds(pl.multiple_of(at, PIECE), PIECE), :] = decay(high, mine) * lo + hi

    loop(half // PIECE, composed)

    def add_meta(k):
        gs[k, rb : rb + 8, :] = both

    loop(M, add_meta)

    def g_copy(k):
        to = lax.rem(chip + 1 + k, M)
        return remote(gs.at[to], gr.at[chip], g_s.at[to], g_r.at[chip], 2 * to + core, s)

    loop(M - 1, lambda k: g_copy(k).start())
    gr[chip] = gs[chip]

    def g_wait(k):
        frm = lax.rem(chip + 1 + k, M)
        remote(gs.at[0], gr.at[frm], g_s.at[frm], g_r.at[frm], 2 * frm + core, s).wait_recv()

    loop(M - 1, g_wait)

    def scan(i):
        at = pl.ds(pl.multiple_of(i * PIECE, PIECE), PIECE)
        speed = rate[pl.ds(pl.multiple_of(core * half + chip * rb + i * PIECE, PIECE), PIECE), :]

        def close(m, carry):
            total, kept, length = carry
            h, d = gr[m, rb : rb + 1, :], gr[m, rb + 1 : rb + 2, :]
            factor = h * jnp.exp(-(speed * d))
            jm[m, at, :] = factor
            return factor * total + gr[m, at, :], kept * h, length + d

        total, kept, length = lax.fori_loop(
            0, M, close,
            (jnp.zeros((PIECE, ny), F32), jnp.ones((1, ny), F32), jnp.zeros((1, ny), F32)),
        )

        def march(m, state):
            is_[m, at, :] = state
            return jm[m, at, :] * state + gr[m, at, :]

        lax.fori_loop(0, M, march, total / (1.0 - kept * jnp.exp(-(speed * length))))

    loop(rb // PIECE, scan)

    def i_copy(k):
        to = lax.rem(chip + 1 + k, M)
        return remote(is_.at[to], ir.at[chip], i_s.at[to], i_r.at[chip], 2 * to + core, s)

    loop(M - 1, lambda k: i_copy(k).start())
    ir[chip] = is_[chip]

    def i_wait(k):
        frm = lax.rem(chip + 1 + k, M)
        remote(is_.at[0], ir.at[frm], i_s.at[frm], i_r.at[frm], 2 * frm + core, s).wait_recv()

    loop(M - 1, i_wait)


    def predict(i):
        block, at = place(i)
        mine, lo, _ = pieces(i)
        p0 = ir[block, pl.ds(pl.multiple_of(at, PIECE), PIECE), :]
        p1 = decay(low, mine) * p0 + lo
        z = core * (nz // 2) + i // (nx // PIECE)
        within = pl.ds(pl.multiple_of(lax.rem(i, nx // PIECE) * PIECE, PIECE), PIECE)
        vb[z + 1, within, :] = jnp.where(core == 0, p0, p1)
        ps[i // (nx // PIECE), within, :] = jnp.where(core == 0, p1, p0)

    loop(half // PIECE, predict)
    beside = lax.rem(s + S - 1 + 2 * core, S)
    edge = (1 - core) * (nz + 1)
    hb = [
        remote(
            vb.at[1 + core * (nz - 1)], vb.at[edge], hb_s.at[0], hb_r.at[1 - core], t, beside
        ),
        remote(
            ps.at[core * (nz // 2 - 1)], vb.at[edge], hb_s.at[1], hb_r.at[1 - core], mate, beside
        ),
    ]
    give = remote(
        ps, vb.at[pl.ds(1 + core * (nz // 2), nz // 2)], pair_s.at[2], pair_r.at[2], mate, s
    )
    for c in hb + [give]:
        c.start()
    fill(vb, 1 + core * (nz // 2), nz // 2)
    give.wait_recv()
    fill(vb, 1 + (1 - core) * (nz // 2), nz // 2)
    for side in range(2):
        remote(
            ps.at[0], vb.at[side * (nz + 1)], hb_s.at[side], hb_r.at[side], t, beside
        ).wait_recv()
    edges(vb)
    q[0] = 0.5 + 0.25 * jnp.tanh(vb[0])
    q[nz + 1] = 0.5 + 0.25 * jnp.tanh(vb[nz + 1])
    shift[1].wait_recv()
    shift[3].wait_recv()

    def second(z):
        c, p = solved(vb, z, temp_sh)
        out[z] = c + p + (vertical(z) - p_sh[z])

    loop(nz, second)

    for c in halo + shift + [mates, swap, give] + hb:
        c.wait_send()
    loop(S, lambda k: c_copy(k).wait_send())
    loop(S - 1, lambda k: e_copy(k).wait_send())
    loop(M - 1, lambda k: g_copy(k).wait_send())
    loop(M - 1, lambda k: i_copy(k).wait_send())


def per_device(T, S, starts, holes, rate, zones, htc, gas, hold, duration, inv_x, inv_y, inv_z):
    _, nz, nx, ny = starts.shape
    xb, M = nx // S, T // 2
    half = nz * nx // 2
    rb = half // M
    vmem = pl.BlockSpec(memory_space=pltpu.VMEM)
    smem = pl.BlockSpec(memory_space=pltpu.SMEM)
    dma = lambda n: pltpu.SemaphoreType.DMA((n,))
    v32 = lambda *shape: pltpu.VMEM(shape, F32)
    result = pl.pallas_call(
        functools.partial(kernel, T, S),
        out_shape=jax.ShapeDtypeStruct((nz, nx, ny), F32),
        in_specs=[vmem, vmem, vmem, vmem, smem, smem, smem, smem, vmem, vmem, vmem],
        out_specs=vmem,
        scratch_shapes=[
            v32(nz + 2, nx, ny), v32(nz + 2, nx, ny), v32(nz + 2, nx, ny),
            pltpu.VMEM((ny, ny), BF16),
            v32(ny, nx), v32(nx, ny), v32(nx, ny), v32(nx, ny),
            v32(8, ny), v32(8, ny), v32(8, ny),
            v32(nz, nx, ny), v32(nz, nx, ny), v32(nz, nx, ny),
            v32(nx * nz, ny),
            pltpu.VMEM((nx, nz, ny), BF16),
            pltpu.VMEM((S, xb, nz, ny), BF16),
            v32(S * nz * xb, ny), v32(S, nz * xb, ny),
            v32(nz * nx, ny), v32(half, ny),
            v32(M, rb + 8, ny), v32(M, rb + 8, ny), v32(M, rb, ny),
            v32(M, rb, ny), v32(M, rb, ny), v32(nz // 2, nx, ny),
            dma(2), dma(2), dma(4), dma(4), dma(S), dma(S), dma(S), dma(S), dma(3), dma(3),
            dma(M), dma(M), dma(M), dma(M), dma(2), dma(2),
        ],
        compiler_params=pltpu.CompilerParams(
            collective_id=0, has_side_effects=True, vmem_limit_bytes=48 * 1024 * 1024
        ),
    )(
        starts[0], holes, rate.reshape(nz * nx, ny), zones.reshape(2 * nz, nx),
        htc, gas, hold, duration, inv_x, inv_y, inv_z,
    )
    return result[None]


def solution(mesh):
    return jax.shard_map(
        functools.partial(per_device, mesh.shape["tm"], mesh.shape["space"]),
        mesh=mesh,
        in_specs=(
            P("tm", "space", None, None),
            P("space", None, None),
            P("space", None, None),
            P(None, "space", None),
            P(),
            P("tm", None),
            P("tm"),
            P("tm"),
            P(),
            P(),
            P(),
        ),
        out_specs=P("tm", "space", None, None),
        check_vma=False,
    )
```

time: 755 us -> 146 us (0.19)
  the two profiles are of different devices: /device:TPU:134 before, /device:TPU:64 now
where the time goes in v1:
time: 146 us
  Pallas kernels  136 us (93%)
  local copies, waits for them, and re-layouts  8.44 us (6%)
    pallas_call x1, Pallas kernels, per_device(): pl.pallas_call(functools.partial(kernel, T, S), out_shape=jax.ShapeDtypeS...  136 us
    unnamed x19, local copies, waits for them, and re-layouts  8.44 us

profile of v1, /device:TPU:64, one launch (start us, length us, event | category | flops | bytes accessed | tf_op | source)
XLA Modules:
  0.0 145.5 jit_solution(7852980503366582346)
XLA Ops:
  1.3 0.0 copy-start.7
  1.3 0.0 copy-start.8
  1.3 0.6 copy-done.7
  2.0 0.0 copy-done.8
  2.0 0.0 copy-start
  2.0 1.2 copy-done
  3.2 0.0 copy-start.1
  3.2 1.2 copy-done.1
  4.4 0.0 copy-start.2
  4.4 1.2 copy-done.2
  5.6 0.0 copy-start.3
  5.6 0.9 copy-done.3
  6.5 0.0 copy-start.4
  6.6 0.8 copy-done.4
  7.3 0.0 copy-start.5
  7.3 0.8 copy-done.5
  8.1 0.0 copy-start.6
  8.1 0.7 copy-done.6
  8.8 135.8 %shard_map.109 = f32[16,128,128]{2,1,0:T(8,128)S(1)} custom-call(f32[16,128,128]{2,1,0:T(8,128)S(1)} %bitcast.5, s32[16,128,128]{2,1,0:T(8,128)S(1)} %copy-done.1, f32[2048,128]{1,0:T(8,128)S(1)} %bitcast.6, s32[32,128]{1,0:T(8,128)S(1)} %bitcast.7, f32[8]{0:T(128)S(1)} %copy-done.7, f32[1,8]{1,0:T(1,128)S(1)} %copy-done.8, f32[1]{0:T(128)S(6)} %copy.13.hold, ...), custom_call_target="tpu_custom_call" | custom-call | tf_op jit(solution)/shard_map/pallas_call | solution.py:356
  144.5 1.0 copy.15
Async XLA Ops:
  1.3 0.7 copy-start.7
  1.3 0.7 copy-start.8
  2.0 1.2 copy-start
  3.2 1.2 copy-start.1
  4.4 1.2 copy-start.2
  5.6 0.9 copy-start.3
  6.5 0.8 copy-start.4
  7.3 0.8 copy-start.5
  8.1 0.7 copy-start.6

commit v2 on v1

v2 whole, which is shorter than its diff:
```python
import functools

import jax
import jax.numpy as jnp
from jax import lax
from jax.experimental import pallas as pl
from jax.experimental.pallas import tpu as pltpu
from jax.sharding import PartitionSpec as P

COOLING = 4.0
COOLANT = -1.0
TIME_STEP = 0.2
MESH = pl.DeviceIdType.MESH
PIECE = 64
F32 = jnp.float32
BF16 = jnp.bfloat16


def loop(count, body):
    lax.fori_loop(0, count, lambda i, c: (body(i), c)[1], 0)


def kernel(
    T, S,
    u_in, holes_in, rate_in, zones_in, htc, gas, hold, duration, inv_x_in, inv_y_in, inv_z_in,
    out,
    u, holes, rate, zones, inv_x, inv_y, inv_z, load_s,
    va, vb, q, iyt, rows_tab, coef_tab, temp_tab, temp_sh, meta, meta_sh, meta_pt,
    u_sh, planar, turned, cs, cr, es, aff, px, ver, ps, jm, gf,
    p_q, p_u, psh_q, psh_u, eq, eu, er_q, er_u, gs_q, gs_u, gr_q, gr_u, is_q, is_u, ir_q, ir_u,
    halo_s, halo_r, shift_s, shift_r, c_s, c_r, e_s, e_r, pair_s, pair_r,
    g_s, g_r, i_s, i_r, hb_s, hb_r,
):
    t, s = lax.axis_index("tm"), lax.axis_index("space")
    core = lax.rem(t, 2)
    chip = t // 2
    M = T // 2
    mate = t + 1 - 2 * core
    nt, pt = lax.rem(t + 1, T), lax.rem(t + T - 1, T)
    down, up = lax.rem(s + S - 1, S), lax.rem(s + 1, S)
    nz, nx, ny = u.shape
    xb = nx // S
    half = nz * nx // 2
    rb = half // M

    def remote(src, dst, send, recv, tt, ss):
        return pltpu.make_async_remote_copy(
            src_ref=src, dst_ref=dst, send_sem=send, recv_sem=recv,
            device_id=(tt, ss), device_id_type=MESH,
        )

    loads = [
        pltpu.make_async_copy(src, dst, load_s.at[i])
        for i, (src, dst) in enumerate(
            (
                (zones_in, zones), (u_in, u), (inv_y_in, inv_y), (inv_x_in, inv_x),
                (holes_in, holes), (rate_in, rate), (inv_z_in, inv_z),
            )
        )
    ]
    for c in loads:
        c.start()

    barrier = pltpu.get_barrier_semaphore()

    def greet(tt, ss):
        pl.semaphore_signal(barrier, inc=1, device_id=(tt, ss), device_id_type=MESH)

    loop(S, lambda k: greet(pt, k))
    loop(S - 1, lambda k: greet(t, lax.rem(s + 1 + k, S)))
    loop(M - 1, lambda k: greet(2 * lax.rem(chip + 1 + k, M) + core, s))
    greet(mate, s)
    greet(mate, lax.rem(s + S - 1 + 2 * core, S))

    number = htc.shape[0]
    loads[0].wait()
    zid = zones[...]
    coef = jnp.zeros(zid.shape, F32)
    temp = jnp.zeros(zid.shape, F32)
    for k in range(number):
        coef = jnp.where(zid == k, htc[k], coef)
        temp = jnp.where(zid == k, gas[0, k], temp)
    for tab, values in ((coef_tab, coef), (temp_tab, temp)):
        rows_tab[...] = jnp.zeros_like(rows_tab)
        for z in range(nz):
            rows_tab[2 * z : 2 * z + 1, :] = values[z : z + 1, :]
            at = (2 * z - 1) % ny
            rows_tab[at : at + 1, :] = values[nz + z : nz + z + 1, :]
        tab[...] = rows_tab[...].T
    meta[0:1, :] = jnp.full((1, ny), hold[0], F32)
    meta[1:2, :] = jnp.full((1, ny), duration[0] * (1.0 / T), F32)
    meta[2:8, :] = jnp.zeros((6, ny), F32)
    for c in loads[1:]:
        c.wait()
    iyt[...] = inv_y[...].astype(F32).T.astype(BF16)

    pl.semaphore_wait(barrier, S + S - 1 + M - 1 + 2)

    halo = [
        remote(u.at[nz - 1], va.at[0], halo_s.at[0], halo_r.at[0], t, up),
        remote(u.at[0], va.at[nz + 1], halo_s.at[1], halo_r.at[1], t, down),
    ]
    shift = [
        remote(meta, meta_sh, shift_s.at[0], shift_r.at[0], nt, s),
        remote(temp_tab, temp_sh, shift_s.at[1], shift_r.at[1], nt, s),
        remote(u, u_sh, shift_s.at[2], shift_r.at[2], nt, s),
        remote(p_q, psh_q, shift_s.at[3], shift_r.at[3], nt, s),
        remote(p_u, psh_u, shift_s.at[4], shift_r.at[4], nt, s),
    ]
    for c in halo + shift[:3]:
        c.start()

    row = lax.broadcasted_iota(jnp.int32, (nx, ny), 0)
    lane = lax.broadcasted_iota(jnp.int32, (nx, ny), 1)

    def conductivity(v):
        return 0.5 + 0.25 * jnp.tanh(v)

    def fill(v, lo, count):
        def one(i):
            q[lo + i] = conductivity(v[lo + i])

        loop(count, one)

    def edges(v):
        v[0] = jnp.where(s > 0, v[0], 0.0)
        v[nz + 1] = jnp.where(s < S - 1, v[nz + 1], 0.0)
        q[0] = conductivity(v[0])
        q[nz + 1] = conductivity(v[nz + 1])

    def solved(v, z, temps):
        c, qc = v[z + 1], q[z + 1]
        outer = (qc + 0.5) * c
        flux = (q[z + 2] + qc) * (v[z + 2] - c) - (q[z] + qc) * (c - v[z])
        for axis, index, last in ((0, row, nx - 1), (1, lane, ny - 1)):
            n = c.shape[axis]
            vn, qn = pltpu.roll(c, n - 1, axis), pltpu.roll(qc, n - 1, axis)
            ahead = jnp.where(index == last, -outer, (qn + qc) * (vn - c))
            behind = jnp.where(index == 0, outer, pltpu.roll(ahead, 1, axis))
            flux = flux + ahead - behind
        turn = lax.rem(ny - 2 * z, ny)
        face_coef = pltpu.roll(coef_tab[...], turn, 1)
        face_temp = pltpu.roll(temps[...], turn, 1)
        on_face = (lane == 0) | (lane == ny - 1)
        surface = jnp.where(on_face, face_coef * (face_temp - c), 0.0)
        cooled = COOLING * holes[z].astype(F32) * (COOLANT - c)
        e = (TIME_STEP * (flux + surface + cooled)).astype(BF16)
        x = jnp.dot(inv_x[...], e, preferred_element_type=F32).astype(BF16)
        return c, jnp.dot(x, iyt[...], preferred_element_type=F32)

    def coded(v):
        top = jnp.max(jnp.abs(v), axis=0, keepdims=True)
        unit = jnp.maximum(top, 1e-30) * (1.0 / 32767.0)
        steps = jnp.round(v * (1.0 / unit))
        return steps.astype(jnp.int32).astype(jnp.int16), unit

    def decoded(steps, unit):
        return steps.astype(jnp.int32).astype(F32) * unit

    def own_copy(i):
        field = u[i]
        va[i + 1] = field
        q[i + 1] = conductivity(field)

    loop(nz, own_copy)

    def keep(z, p):
        planar[z] = p
        turned[pl.ds(z, nx, stride=nz), :] = p

    def first(i):
        z = 1 + 2 * i
        _, p = solved(va, z, temp_tab)
        _, r = solved(va, z + 1, temp_tab)
        keep(z, p)
        keep(z + 1, r)

    loop((nz - 2) // 2, first)
    halo[0].wait_recv()
    halo[1].wait_recv()
    edges(va)
    for z in (0, nz - 1):
        keep(z, solved(va, z, temp_tab)[1])

    def c_copy(k):
        to = lax.rem(s + 1 + k, S)
        return remote(
            cs.at[pl.ds(to * xb, xb)], cr.at[s], c_s.at[to], c_r.at[s], t, to
        )

    def c_block(to):
        block = turned[pl.ds(to * (xb * nz), xb * nz), :]
        return block.reshape(xb, nz, ny).astype(BF16)

    def c_send(k):
        to = lax.rem(s + 1 + k, S)
        cs[pl.ds(to * xb, xb)] = c_block(to)
        c_copy(k).start()

    loop(S - 1, c_send)
    cr[s] = c_block(s)

    def p_code(z):
        p_q[z], p_u[z] = coded(planar[z])

    loop(nz, p_code)
    shift[3].start()
    shift[4].start()
    shift[0].wait_recv()
    mates = remote(meta_sh, meta_pt, pair_s.at[0], pair_r.at[0], mate, s)
    mates.start()
    shift[2].wait_recv()
    per = PIECE // xb

    def decay(m, rows):
        return m[0:1, :] * jnp.exp(-(rate[rows, :] * m[1:2, :]))

    def base(i):
        field = u_sh[i]
        rows = pl.ds(pl.multiple_of(i * nx, nx), nx)
        aff[i] = (field - decay(meta_sh, rows) * field).reshape(S, xb, ny)

    loop(nz, base)

    def c_wait(k):
        frm = lax.rem(s + 1 + k, S)
        remote(cs.at[pl.ds(0, xb)], cr.at[frm], c_s.at[frm], c_r.at[frm], t, frm).wait_recv()

    loop(S - 1, c_wait)
    for x in range(xb):
        lines = cr[:, x].reshape(S * nz, ny)
        es[pl.ds(x, S * nz, stride=xb), :] = jnp.dot(
            inv_z[...], lines, preferred_element_type=F32
        )

    blk = nz * xb

    def e_copies(k):
        to = lax.rem(s + 1 + k, S)
        return (
            remote(eq.at[to], er_q.at[s], e_s.at[to], e_r.at[s], nt, to),
            remote(eu.at[to], er_u.at[s], e_s.at[S + to], e_r.at[S + s], nt, to),
        )

    def e_send(k):
        to = lax.rem(s + 1 + k, S)
        eq[to], eu[to] = coded(es[pl.ds(pl.multiple_of(to * blk, blk), blk), :])
        for c in e_copies(k):
            c.start()

    loop(S, e_send)

    def e_take(k):
        frm = lax.rem(s + 1 + k, S)
        remote(eq.at[0], er_q.at[frm], e_s.at[frm], e_r.at[frm], nt, frm).wait_recv()
        remote(eu.at[0], er_u.at[frm], e_s.at[frm], e_r.at[S + frm], nt, frm).wait_recv()
        part = decoded(er_q[frm], er_u[frm]).reshape(nz, xb, ny)
        ver[:, frm] = part
        aff[:, frm] = aff[:, frm] + part

    loop(S, e_take)
    swap = remote(
        aff.at[pl.ds((1 - core) * (nz // 2), nz // 2)], px, pair_s.at[1], pair_r.at[1], mate, s
    )
    swap.start()
    mates.wait_recv()
    low = jnp.where(core == 0, meta_sh[...], meta_pt[...])
    high = jnp.where(core == 0, meta_pt[...], meta_sh[...])
    swap.wait_recv()

    def pieces(i):
        mine = pl.ds(pl.multiple_of(core * half + i * PIECE, PIECE), PIECE)
        z, at = i // (nx // PIECE), lax.rem(i, nx // PIECE) * per
        own = aff[core * (nz // 2) + z, pl.ds(at, per)].reshape(PIECE, ny)
        other = px[z, pl.ds(at, per)].reshape(PIECE, ny)
        return mine, jnp.where(core == 0, own, other), jnp.where(core == 0, other, own)

    each = rb // PIECE

    def g_copies(k):
        to = lax.rem(chip + 1 + k, M)
        there = 2 * to + core
        return (
            remote(gs_q.at[to], gr_q.at[chip], g_s.at[to], g_r.at[chip], there, s),
            remote(gs_u.at[to], gr_u.at[chip], g_s.at[M + to], g_r.at[M + chip], there, s),
        )

    def g_block(to):
        for j in range(each):
            mine, lo, hi = pieces(to * each + j)
            steps, unit = coded(decay(high, mine) * lo + hi)
            gs_q[to, j] = steps
            gs_u[to, j] = jnp.concatenate(
                [low[0:1] * high[0:1], low[1:2] + high[1:2], unit, unit], axis=0
            )

    def g_send(k):
        g_block(lax.rem(chip + 1 + k, M))
        for c in g_copies(k):
            c.start()

    loop(M - 1, g_send)
    g_block(chip)
    gr_q[chip] = gs_q[chip]
    gr_u[chip] = gs_u[chip]

    def speed(j):
        return rate[pl.ds(pl.multiple_of(core * half + chip * rb + j * PIECE, PIECE), PIECE), :]

    def g_wait(k):
        frm = lax.rem(chip + 1 + k, M)
        there = 2 * frm + core
        remote(gs_q.at[0], gr_q.at[frm], g_s.at[frm], g_r.at[frm], there, s).wait_recv()
        remote(gs_u.at[0], gr_u.at[frm], g_s.at[frm], g_r.at[M + frm], there, s).wait_recv()

    shift[1].wait_recv()
    shift[3].wait_recv()
    shift[4].wait_recv()

    def defect(z):
        ver[z] = ver[z] - decoded(psh_q[z], psh_u[z]).reshape(S, xb, ny)

    loop(nz, defect)
    loop(M - 1, g_wait)

    def i_copies(to):
        there = 2 * to + core
        return (
            remote(is_q.at[to], ir_q.at[chip], i_s.at[to], i_r.at[chip], there, s),
            remote(is_u.at[to], ir_u.at[chip], i_s.at[M + to], i_r.at[M + chip], there, s),
        )

    totals = []
    for j in range(each):

        def close(m, carry, j=j):
            total, kept, length = carry
            h, d = gr_u[m, j, 0:1], gr_u[m, j, 1:2]
            factor = h * jnp.exp(-(speed(j) * d))
            term = decoded(gr_q[m, j], gr_u[m, j, 2:3])
            jm[m, j] = factor
            gf[m, j] = term
            return factor * total + term, kept * h, length + d

        total, kept, length = lax.fori_loop(
            0, M, close,
            (jnp.zeros((PIECE, ny), F32), jnp.ones((1, ny), F32), jnp.zeros((1, ny), F32)),
        )
        totals.append(total / (1.0 - kept * jnp.exp(-(speed(j) * length))))

    def march(m, states):
        for j in range(each):
            is_q[m, j], is_u[m, j] = coded(states[j])

        @pl.when(m != chip)
        def _():
            for c in i_copies(m):
                c.start()

        return tuple(jm[m, j] * states[j] + gf[m, j] for j in range(each))

    lax.fori_loop(0, M, march, tuple(totals))
    ir_q[chip] = is_q[chip]
    ir_u[chip] = is_u[chip]

    def predict(i):
        block, j = i // each, lax.rem(i, each)
        mine, lo, _ = pieces(i)
        p0 = decoded(ir_q[block, j], ir_u[block, j])
        p1 = decay(low, mine) * p0 + lo
        z = i // (nx // PIECE)
        within = pl.ds(pl.multiple_of(lax.rem(i, nx // PIECE) * PIECE, PIECE), PIECE)
        kept = jnp.where(core == 0, p0, p1)
        vb[core * (nz // 2) + z + 1, within, :] = kept
        q[core * (nz // 2) + z + 1, within, :] = conductivity(kept)
        ps[z, within, :] = jnp.where(core == 0, p1, p0)

    def i_take(k):
        frm = lax.rem(chip + 1 + k, M)
        there = 2 * frm + core
        remote(is_q.at[0], ir_q.at[frm], i_s.at[frm], i_r.at[frm], there, s).wait_recv()
        remote(is_u.at[0], ir_u.at[frm], i_s.at[frm], i_r.at[M + frm], there, s).wait_recv()
        for j in range(each):
            predict(frm * each + j)

    loop(M - 1, i_take)
    for j in range(each):
        predict(chip * each + j)
    beside = lax.rem(s + S - 1 + 2 * core, S)
    edge = (1 - core) * (nz + 1)
    hb = [
        remote(
            ps.at[core * (nz // 2 - 1)], vb.at[edge], hb_s.at[1], hb_r.at[1 - core], mate, beside
        ),
        remote(
            vb.at[1 + core * (nz - 1)], vb.at[edge], hb_s.at[0], hb_r.at[1 - core], t, beside
        ),
    ]
    give = remote(
        ps, vb.at[pl.ds(1 + core * (nz // 2), nz // 2)], pair_s.at[2], pair_r.at[2], mate, s
    )
    for c in hb + [give]:
        c.start()

    def second(i):
        z0 = lax.rem(core * (nz // 2) + 1 + 2 * i, nz)
        z1 = lax.rem(core * (nz // 2) + 2 + 2 * i, nz)
        c0, p = solved(vb, z0, temp_sh)
        c1, r = solved(vb, z1, temp_sh)
        out[z0] = c0 + p + ver[z0].reshape(nx, ny)
        out[z1] = c1 + r + ver[z1].reshape(nx, ny)

    inner = nz // 4 - 1
    loop(inner, second)
    give.wait_recv()
    fill(vb, 1 + (1 - core) * (nz // 2), nz // 2)
    for side in range(2):
        remote(
            ps.at[0], vb.at[side * (nz + 1)], hb_s.at[side], hb_r.at[side], t, beside
        ).wait_recv()
    edges(vb)
    loop(nz // 2 - inner, lambda i: second(i + inner))

    for c in halo + shift + [mates, swap, give] + hb:
        c.wait_send()
    loop(S - 1, lambda k: c_copy(k).wait_send())

    def sent(copies):
        for c in copies:
            c.wait_send()

    loop(S, lambda k: sent(e_copies(k)))
    loop(M - 1, lambda k: sent(g_copies(k)))
    loop(M - 1, lambda k: sent(i_copies(lax.rem(chip + 1 + k, M))))


def per_device(T, S, starts, holes, rate, zones, htc, gas, hold, duration, inv_x, inv_y, inv_z):
    _, nz, nx, ny = starts.shape
    xb, M = nx // S, T // 2
    half = nz * nx // 2
    each = half // M // PIECE
    vmem = pl.BlockSpec(memory_space=pltpu.VMEM)
    hbm = pl.BlockSpec(memory_space=pltpu.HBM)
    smem = pl.BlockSpec(memory_space=pltpu.SMEM)
    dma = lambda n: pltpu.SemaphoreType.DMA((n,))
    i16 = lambda *shape: pltpu.VMEM(shape, jnp.int16)
    v32 = lambda *shape: pltpu.VMEM(shape, F32)
    result = pl.pallas_call(
        functools.partial(kernel, T, S),
        out_shape=jax.ShapeDtypeStruct((nz, nx, ny), F32),
        in_specs=[hbm, hbm, hbm, hbm, smem, smem, smem, smem, hbm, hbm, hbm],
        out_specs=vmem,
        scratch_shapes=[
            v32(nz, nx, ny), pltpu.VMEM((nz, nx, ny), jnp.int32), v32(nz * nx, ny),
            pltpu.VMEM((2 * nz, nx), jnp.int32), pltpu.VMEM((nx, nx), BF16),
            pltpu.VMEM((ny, ny), BF16), pltpu.VMEM((S * nz, S * nz), BF16), dma(7),
            v32(nz + 2, nx, ny), v32(nz + 2, nx, ny), v32(nz + 2, nx, ny),
            pltpu.VMEM((ny, ny), BF16),
            v32(ny, nx), v32(nx, ny), v32(nx, ny), v32(nx, ny),
            v32(8, ny), v32(8, ny), v32(8, ny),
            v32(nz, nx, ny), v32(nz, nx, ny), v32(nx * nz, ny),
            pltpu.VMEM((nx, nz, ny), BF16), pltpu.VMEM((S, xb, nz, ny), BF16),
            v32(S * nz * xb, ny), v32(nz, S, xb, ny), v32(nz // 2, S, xb, ny),
            v32(nz, S, xb, ny), v32(nz // 2, nx, ny),
            v32(M, each, PIECE, ny), v32(M, each, PIECE, ny),
            i16(nz, nx, ny), v32(nz, 1, ny), i16(nz, nx, ny), v32(nz, 1, ny),
            i16(S, nz * xb, ny), v32(S, 1, ny), i16(S, nz * xb, ny), v32(S, 1, ny),
            i16(M, each, PIECE, ny), v32(M, each, 4, ny), i16(M, each, PIECE, ny), v32(M, each, 4, ny),
            i16(M, each, PIECE, ny), v32(M, each, 1, ny), i16(M, each, PIECE, ny), v32(M, each, 1, ny),
            dma(2), dma(2), dma(5), dma(5), dma(S), dma(S), dma(2 * S), dma(2 * S), dma(3), dma(3),
            dma(2 * M), dma(2 * M), dma(2 * M), dma(2 * M), dma(2), dma(2),
        ],
        compiler_params=pltpu.CompilerParams(
            collective_id=0, has_side_effects=True, vmem_limit_bytes=60 * 1024 * 1024
        ),
    )(
        starts[0], holes, rate.reshape(nz * nx, ny), zones.reshape(2 * nz, nx),
        htc, gas, hold, duration, inv_x, inv_y, inv_z,
    )
    return result[None]


def solution(mesh):
    return jax.shard_map(
        functools.partial(per_device, mesh.shape["tm"], mesh.shape["space"]),
        mesh=mesh,
        in_specs=(
            P("tm", "space", None, None),
            P("space", None, None),
            P("space", None, None),
            P(None, "space", None),
            P(),
            P("tm", None),
            P("tm"),
            P("tm"),
            P(),
            P(),
            P(),
        ),
        out_specs=P("tm", "space", None, None),
        check_vma=False,
    )
```

time: 146 us -> 103 us (0.71)
  the two profiles are of different devices: /device:TPU:64 before, /device:TPU:70 now
where the time goes in v2:
time: 103 us
  Pallas kernels  99.6 us (97%)
  local copies, waits for them, and re-layouts  2.3 us (2%)
  between operations  1.3 us (1%)
    pallas_call x1, Pallas kernels, per_device(): pl.pallas_call(functools.partial(kernel, T, S), out_shape=jax.ShapeDtypeS...  99.6 us
    unnamed x1, local copies, waits for them, and re-layouts  2.3 us

profile of v2, /device:TPU:70, one launch (start us, length us, event | category | flops | bytes accessed | tf_op | source)
XLA Modules:
  0.0 103.2 jit_solution(7208987922502701609)
XLA Ops:
  1.3 99.6 %shard_map.109 = f32[16,128,128]{2,1,0:T(8,128)} custom-call(f32[16,128,128]{2,1,0:T(8,128)} %bitcast.5, s32[16,128,128]{2,1,0:T(8,128)} %holes_in.1, f32[2048,128]{1,0:T(8,128)} %bitcast.6, s32[32,128]{1,0:T(8,128)} %bitcast.7, f32[8]{0:T(128)} %htc.1, f32[1,8]{1,0:T(1,128)} %gas.1, f32[1]{0:T(128)S(6)} %copy.13.hold, f32[1]{0:T(128)S(6)} %copy.14.duration, ...), custom_call_target="tpu_custom_call" | custom-call | tf_op jit(solution)/shard_map/pallas_call | solution.py:448
  100.9 2.3 %copy.15 = f32[1,16,128,128]{3,2,1,0:T(8,128)} copy(f32[1,16,128,128]{3,2,1,0:T(8,128)} %bitcast.4) | data formatting | bytes 2097152

commit v3 on v2

v3 whole, which is shorter than its diff:
```python
import functools

import jax
import jax.numpy as jnp
from jax import lax
from jax.experimental import pallas as pl
from jax.experimental.pallas import tpu as pltpu
from jax.sharding import PartitionSpec as P

COOLING = 4.0
COOLANT = -1.0
TIME_STEP = 0.2
MESH = pl.DeviceIdType.MESH
F32 = jnp.float32
BF16 = jnp.bfloat16


def loop(count, body):
    lax.fori_loop(0, count, lambda i, c: (body(i), c)[1], 0)


def kernel(
    T, S,
    u_in, holes_in, rate_in, zones_in, htc, gas, hold, duration, inv_x_in, inv_y_in, inv_z_in,
    out_q, out_u,
    u, holes, rate, zones, inv_x, inv_y, inv_z, load_s,
    va, vb, q, iyt, rows_tab, coef_tab, temp_tab, meta, meta_pt,
    planar, turned, cs, cr, es, aff, px, ver, ps, jm, gf,
    eq, eu, er_q, er_u, gs_q, gs_u, gr_q, gr_u, is_q, is_u, ir_q, ir_u, oq, ou,
    halo_s, halo_r, meta_s, meta_r, c_s, c_r, e_s, e_r, swap_s, swap_r,
    g_s, g_r, i_s, i_r, give_s, give_r, hb_s, hb_r, o_s, o_r,
):
    t, s = lax.axis_index("tm"), lax.axis_index("space")
    core = lax.rem(t, 2)
    chip = t // 2
    M, H = T // 2, S // 2
    mate = t + 1 - 2 * core
    nt, pt = lax.rem(t + 1, T), lax.rem(t + T - 1, T)
    down, up = lax.rem(s + S - 1, S), lax.rem(s + 1, S)
    nz, nx, ny = u.shape
    xb = nx // S
    blk = nz * xb
    rb = nz * nx // 2 // M
    zr = rb // xb
    ratio = blk // rb
    base_x = core * (nx // 2)

    def remote(src, dst, send, recv, tt, ss):
        return pltpu.make_async_remote_copy(
            src_ref=src, dst_ref=dst, send_sem=send, recv_sem=recv,
            device_id=(tt, ss), device_id_type=MESH,
        )

    loads = [
        pltpu.make_async_copy(src, dst, load_s.at[i])
        for i, (src, dst) in enumerate(
            (
                (u_in, u), (zones_in, zones), (inv_y_in, inv_y), (inv_x_in, inv_x),
                (holes_in, holes), (rate_in, rate), (inv_z_in, inv_z),
            )
        )
    ]
    for c in loads:
        c.start()

    barrier = pltpu.get_barrier_semaphore()

    def greet(tt, ss):
        pl.semaphore_signal(barrier, inc=1, device_id=(tt, ss), device_id_type=MESH)

    loop(S - 1, lambda k: greet(t, lax.rem(s + 1 + k, S)))
    loop(M - 1, lambda k: greet(2 * lax.rem(chip + 1 + k, M) + core, s))
    greet(mate, s)
    greet(mate, down)
    greet(mate, up)
    greet(pt, s)
    loads[0].wait()
    pl.semaphore_wait(barrier, S - 1 + M - 1 + 4)

    halo = [
        remote(u.at[nz - 1], va.at[0], halo_s.at[0], halo_r.at[0], t, up),
        remote(u.at[0], va.at[nz + 1], halo_s.at[1], halo_r.at[1], t, down),
    ]
    for c in halo:
        c.start()
    meta[0:1, :] = jnp.full((1, ny), hold[0], F32)
    meta[1:2, :] = jnp.full((1, ny), duration[0] * (1.0 / T), F32)
    meta[2:8, :] = jnp.zeros((6, ny), F32)
    mates = remote(meta, meta_pt, meta_s.at[0], meta_r.at[0], mate, s)
    mates.start()

    for c in loads[1:]:
        c.wait()
    zid = zones[...]
    coef = jnp.zeros(zid.shape, F32)
    temp = jnp.zeros(zid.shape, F32)
    for k in range(htc.shape[0]):
        coef = jnp.where(zid == k, htc[k], coef)
        temp = jnp.where(zid == k, gas[0, k], temp)
    for tab, values in ((coef_tab, coef), (temp_tab, temp)):
        rows_tab[...] = jnp.zeros_like(rows_tab)
        for z in range(nz):
            rows_tab[2 * z : 2 * z + 1, :] = values[z : z + 1, :]
            at = (2 * z - 1) % ny
            rows_tab[at : at + 1, :] = values[nz + z : nz + z + 1, :]
        tab[...] = rows_tab[...].T
    iyt[...] = inv_y[...].astype(F32).T.astype(BF16)

    row = lax.broadcasted_iota(jnp.int32, (nx, ny), 0)
    lane = lax.broadcasted_iota(jnp.int32, (nx, ny), 1)

    def conductivity(v):
        return 0.5 + 0.25 * jnp.tanh(v)

    def edges(v):
        v[0] = jnp.where(s > 0, v[0], 0.0)
        v[nz + 1] = jnp.where(s < S - 1, v[nz + 1], 0.0)
        q[0] = conductivity(v[0])
        q[nz + 1] = conductivity(v[nz + 1])

    def solved(v, z):
        c, qc = v[z + 1], q[z + 1]
        outer = (qc + 0.5) * c
        flux = (q[z + 2] + qc) * (v[z + 2] - c) - (q[z] + qc) * (c - v[z])
        for axis, index, last in ((0, row, nx - 1), (1, lane, ny - 1)):
            n = c.shape[axis]
            vn, qn = pltpu.roll(c, n - 1, axis), pltpu.roll(qc, n - 1, axis)
            ahead = jnp.where(index == last, -outer, (qn + qc) * (vn - c))
            behind = jnp.where(index == 0, outer, pltpu.roll(ahead, 1, axis))
            flux = flux + ahead - behind
        turn = lax.rem(ny - 2 * z, ny)
        face_coef = pltpu.roll(coef_tab[...], turn, 1)
        face_temp = pltpu.roll(temp_tab[...], turn, 1)
        on_face = (lane == 0) | (lane == ny - 1)
        surface = jnp.where(on_face, face_coef * (face_temp - c), 0.0)
        cooled = COOLING * holes[z].astype(F32) * (COOLANT - c)
        e = (TIME_STEP * (flux + surface + cooled)).astype(BF16)
        x = jnp.dot(inv_x[...], e, preferred_element_type=F32).astype(BF16)
        return c, jnp.dot(x, iyt[...], preferred_element_type=F32)

    def coded(v):
        top = jnp.max(jnp.abs(v), axis=0, keepdims=True)
        unit = jnp.maximum(top, 1e-30) * (1.0 / 32767.0)
        steps = jnp.round(v * (1.0 / unit))
        return steps.astype(jnp.int32).astype(jnp.int16), unit

    def decoded(steps, unit):
        return steps.astype(jnp.int32).astype(F32) * unit

    def own_copy(i):
        field = u[i]
        va[i + 1] = field
        q[i + 1] = conductivity(field)

    loop(nz, own_copy)

    def keep(z, p):
        planar[z] = p
        turned[pl.ds(z, nx, stride=nz), :] = p

    def first(i):
        z = 1 + 2 * i
        _, p = solved(va, z)
        _, r = solved(va, z + 1)
        keep(z, p)
        keep(z + 1, r)

    loop((nz - 2) // 2, first)
    halo[0].wait_recv()
    halo[1].wait_recv()
    edges(va)
    p, r = solved(va, 0)[1], solved(va, nz - 1)[1]
    keep(0, p)
    keep(nz - 1, r)

    def c_copy(k):
        to = lax.rem(s + 1 + k, S)
        return remote(
            cs.at[pl.ds(to * xb, xb)], cr.at[s], c_s.at[to], c_r.at[s], t, to
        )

    def c_block(to):
        block = turned[pl.ds(to * blk, blk), :]
        return block.reshape(xb, nz, ny).astype(BF16)

    def c_send(k):
        to = lax.rem(s + 1 + k, S)
        cs[pl.ds(to * xb, xb)] = c_block(to)
        c_copy(k).start()

    loop(S - 1, c_send)
    cr[s] = c_block(s)

    def decay(m, speed):
        return m[0:1, :] * jnp.exp(-(speed * m[1:2, :]))

    def lines(ref, k):
        return ref[:, pl.ds(pl.multiple_of(k * xb, xb), xb), :].reshape(blk, ny)

    def base(k):
        field = lines(u, k)
        aff[k] = field - decay(meta, lines(rate, k)) * field

    loop(S, base)
    mates.wait_recv()
    low = jnp.where(core == 0, meta[...], meta_pt[...])
    high = jnp.where(core == 0, meta_pt[...], meta[...])

    def c_wait(k):
        frm = lax.rem(s + 1 + k, S)
        remote(cs.at[pl.ds(0, xb)], cr.at[frm], c_s.at[frm], c_r.at[frm], t, frm).wait_recv()

    loop(S - 1, c_wait)
    for x in range(xb):
        es[pl.ds(x, S * nz, stride=xb), :] = jnp.dot(
            inv_z[...], cr[:, x].reshape(S * nz, ny), preferred_element_type=F32
        )

    def solution_of(k):
        return es[pl.ds(pl.multiple_of(k * blk, blk), blk), :]

    def e_copies(to):
        return (
            remote(eq.at[to], er_q.at[s], e_s.at[to], e_r.at[s], t, to),
            remote(eu.at[to], er_u.at[s], e_s.at[S + to], e_r.at[S + s], t, to),
        )

    def e_send(k):
        to = lax.rem(s + 1 + k, S)
        eq[to], eu[to] = coded(solution_of(to))
        for c in e_copies(to):
            c.start()

    loop(S - 1, e_send)

    def swap(k):
        return remote(
            aff.at[k], px.at[lax.rem(k, H)],
            swap_s.at[lax.rem(k, H)], swap_r.at[lax.rem(k, H)], mate, s,
        )

    def g_copies(to):
        there = 2 * to + core
        return (
            remote(gs_q.at[to], gr_q.at[chip], g_s.at[to], g_r.at[chip], there, s),
            remote(gs_u.at[to], gr_u.at[chip], g_s.at[M + to], g_r.at[M + chip], there, s),
        )

    def maps(k, rows):
        own, other = aff[k, rows, :], px[lax.rem(k, H), rows, :]
        return jnp.where(core == 0, own, other), jnp.where(core == 0, other, own)

    def take(frm, part):
        ver[frm] = part
        aff[frm] = aff[frm] + part

        @pl.when(frm // H != core)
        def _():
            swap(frm).start()

    def e_take(k):
        frm = lax.rem(s + S - 1 - k, S)
        remote(eq.at[0], er_q.at[frm], e_s.at[frm], e_r.at[frm], t, frm).wait_recv()
        remote(eu.at[0], er_u.at[frm], e_s.at[frm], e_r.at[S + frm], t, frm).wait_recv()
        take(frm, decoded(er_q[frm], er_u[frm]))

    def composed(k):
        frm = lax.rem(s + S - k, S)

        @pl.when(frm // H == core)
        def _():
            swap(frm).wait_recv()
            speed = lines(rate, frm)
            for r in range(ratio):
                block = lax.rem(frm, H) * ratio + r
                lo, hi = maps(frm, slice(r * rb, r * rb + rb))
                steps, unit = coded(decay(high, speed[r * rb : r * rb + rb]) * lo + hi)
                gs_q[block] = steps
                gs_u[block] = jnp.concatenate(
                    [low[0:1] * high[0:1], low[1:2] + high[1:2], unit, unit], axis=0
                )

                @pl.when(block != chip)
                def _():
                    for c in g_copies(block):
                        c.start()

    take(s, solution_of(s))
    e_take(0)

    def stream(k):
        e_take(k + 1)
        composed(k)

    loop(S - 2, stream)
    composed(S - 2)
    composed(S - 1)
    gr_q[chip] = gs_q[chip]
    gr_u[chip] = gs_u[chip]

    def plane(ref, z):
        return ref[:, pl.ds(pl.multiple_of(z * xb, xb), xb), :]

    def defect(z):
        rows = pl.ds(pl.multiple_of(z * xb, xb), xb)
        ver[:, rows, :] = ver[:, rows, :] - planar[z].reshape(S, xb, ny)

    loop(nz, defect)

    def cells(ref, block):
        k, r = core * H + block // ratio, lax.rem(block, ratio)
        return ref.at[pl.ds(r * zr, zr), pl.ds(pl.multiple_of(k * xb, xb), xb)]

    def i_copies(to):
        there = 2 * to + core
        return (
            remote(is_q.at[to], ir_q.at[chip], i_s.at[to], i_r.at[chip], there, s),
            remote(is_u.at[to], ir_u.at[chip], i_s.at[M + to], i_r.at[M + chip], there, s),
        )

    speed = cells(rate, chip)[...].reshape(rb, ny)

    def close(m, carry):
        total, kept, length = carry

        @pl.when(m != chip)
        def _():
            there = 2 * m + core
            remote(gs_q.at[0], gr_q.at[m], g_s.at[m], g_r.at[m], there, s).wait_recv()
            remote(gs_u.at[0], gr_u.at[m], g_s.at[m], g_r.at[M + m], there, s).wait_recv()

        h, d = gr_u[m, 0:1], gr_u[m, 1:2]
        factor = h * jnp.exp(-(speed * d))
        term = decoded(gr_q[m], gr_u[m, 2:3])
        jm[m] = factor
        gf[m] = term
        return factor * total + term, kept * h, length + d

    total, kept, length = lax.fori_loop(
        0, M, close,
        (jnp.zeros((rb, ny), F32), jnp.ones((1, ny), F32), jnp.zeros((1, ny), F32)),
    )

    def march(m, state):
        is_q[m], is_u[m] = coded(state)

        @pl.when(m != chip)
        def _():
            for c in i_copies(m):
                c.start()

        return jm[m] * state + gf[m]

    lax.fori_loop(0, M, march, total / (1.0 - kept * jnp.exp(-(speed * length))))

    def give(block):
        return remote(
            cells(ps, block), cells(vb.at[pl.ds(1, nz)], block),
            give_s.at[block], give_r.at[block], mate, s,
        )

    def predict(block, p0):
        k, r = core * H + block // ratio, lax.rem(block, ratio)
        lo, _ = maps(k, pl.ds(pl.multiple_of(r * rb, rb), rb))
        p1 = decay(low, cells(rate, block)[...].reshape(rb, ny)) * p0 + lo
        mine = jnp.where(core == 0, p0, p1).reshape(zr, xb, ny)
        there = (pl.ds(r * zr, zr), pl.ds(pl.multiple_of(k * xb, xb), xb))
        here = (pl.ds(1 + r * zr, zr), pl.ds(pl.multiple_of(k * xb, xb), xb))
        vb[here] = mine
        q[here] = conductivity(mine)
        ps[there] = jnp.where(core == 0, p1, p0).reshape(zr, xb, ny)
        give(block).start()

    predict(chip, decoded(is_q[chip], is_u[chip]))

    def i_take(k):
        frm = lax.rem(chip + 1 + k, M)
        there = 2 * frm + core
        remote(is_q.at[0], ir_q.at[frm], i_s.at[frm], i_r.at[frm], there, s).wait_recv()
        remote(is_u.at[0], ir_u.at[frm], i_s.at[frm], i_r.at[M + frm], there, s).wait_recv()
        predict(frm, decoded(ir_q[frm], ir_u[frm]))

    loop(M - 1, i_take)
    xs = pl.ds(pl.multiple_of(base_x, nx // 2), nx // 2)
    hb = []
    for i, (src, z, side, to) in enumerate(
        (
            (ps, 0, 1, down), (ps, nz - 1, 0, up), (vb, 1, 1, down), (vb, nz, 0, up),
        )
    ):
        hb.append(
            remote(
                src.at[z, xs], vb.at[side * (nz + 1), xs],
                hb_s.at[i], hb_r.at[2 * side + core], mate if i < 2 else t, to,
            )
        )
    for c in hb:
        c.start()

    def give_take(k):
        frm = lax.rem(chip + k, M)
        x = (1 - core) * H + frm // ratio
        where = (pl.ds(1 + lax.rem(frm, ratio) * zr, zr), pl.ds(pl.multiple_of(x * xb, xb), xb))
        remote(cells(ps, frm), vb.at[where], give_s.at[frm], give_r.at[frm], mate, s).wait_recv()
        q[where] = conductivity(vb[where])

    loop(M, give_take)

    def o_copies(z):
        return (
            remote(oq.at[z], out_q.at[z], o_s.at[z], o_r.at[z], nt, s),
            remote(ou.at[z], out_u.at[z], o_s.at[nz + z], o_r.at[nz + z], nt, s),
        )

    def second(z0, z1):
        c0, p = solved(vb, z0)
        c1, r = solved(vb, z1)
        oq[z0], ou[z0] = coded(c0 + p + plane(ver, z0).reshape(nx, ny))
        oq[z1], ou[z1] = coded(c1 + r + plane(ver, z1).reshape(nx, ny))
        for c in o_copies(z0) + o_copies(z1):
            c.start()

    loop((nz - 2) // 2, lambda i: second(1 + 2 * i, 2 + 2 * i))
    for side in range(2):
        for c in range(2):
            remote(
                ps.at[0, xs], vb.at[side * (nz + 1), pl.ds(c * (nx // 2), nx // 2)],
                hb_s.at[0], hb_r.at[2 * side + c], t, down,
            ).wait_recv()
    edges(vb)
    second(0, nz - 1)

    def sent(copies):
        for c in copies:
            c.wait_send()

    sent(halo + [mates] + hb)
    loop(S - 1, lambda k: c_copy(k).wait_send())
    loop(S - 1, lambda k: sent(e_copies(lax.rem(s + 1 + k, S))))
    loop(H, lambda k: swap((1 - core) * H + k).wait_send())
    loop(M - 1, lambda k: sent(g_copies(lax.rem(chip + 1 + k, M))))
    loop(M - 1, lambda k: sent(i_copies(lax.rem(chip + 1 + k, M))))
    loop(M, lambda k: give(k).wait_send())

    def arrived(z):
        for c in o_copies(z):
            c.wait()

    loop(nz, arrived)


def per_device(T, S, starts, holes, rate, zones, htc, gas, hold, duration, inv_x, inv_y, inv_z):
    _, nz, nx, ny = starts.shape
    xb, M = nx // S, T // 2
    blk, rb = nz * xb, nz * nx // 2 // M
    hbm = pl.BlockSpec(memory_space=pltpu.HBM)
    smem = pl.BlockSpec(memory_space=pltpu.SMEM)
    dma = lambda n: pltpu.SemaphoreType.DMA((n,))
    i16 = lambda *shape: pltpu.VMEM(shape, jnp.int16)
    v32 = lambda *shape: pltpu.VMEM(shape, F32)
    steps, unit = pl.pallas_call(
        functools.partial(kernel, T, S),
        out_shape=(
            jax.ShapeDtypeStruct((nz, nx, ny), jnp.int16),
            jax.ShapeDtypeStruct((nz, 1, ny), F32),
        ),
        in_specs=[hbm, hbm, hbm, hbm, smem, smem, smem, smem, hbm, hbm, hbm],
        out_specs=(hbm, hbm),
        scratch_shapes=[
            v32(nz, nx, ny), pltpu.VMEM((nz, nx, ny), jnp.int32), v32(nz, nx, ny),
            pltpu.VMEM((2 * nz, nx), jnp.int32), pltpu.VMEM((nx, nx), BF16),
            pltpu.VMEM((ny, ny), BF16), pltpu.VMEM((S * nz, S * nz), BF16), dma(7),
            v32(nz + 2, nx, ny), v32(nz + 2, nx, ny), v32(nz + 2, nx, ny),
            pltpu.VMEM((ny, ny), BF16),
            v32(ny, nx), v32(nx, ny), v32(nx, ny),
            v32(8, ny), v32(8, ny),
            v32(nz, nx, ny), v32(nx * nz, ny),
            pltpu.VMEM((nx, nz, ny), BF16), pltpu.VMEM((S, xb, nz, ny), BF16),
            v32(S * blk, ny), v32(S, blk, ny), v32(S // 2, blk, ny),
            v32(S, blk, ny), v32(nz, nx, ny),
            v32(M, rb, ny), v32(M, rb, ny),
            i16(S, blk, ny), v32(S, 1, ny), i16(S, blk, ny), v32(S, 1, ny),
            i16(M, rb, ny), v32(M, 4, ny), i16(M, rb, ny), v32(M, 4, ny),
            i16(M, rb, ny), v32(M, 1, ny), i16(M, rb, ny), v32(M, 1, ny),
            i16(nz, nx, ny), v32(nz, 1, ny),
            dma(2), dma(2), dma(1), dma(1), dma(S), dma(S), dma(2 * S), dma(2 * S),
            dma(S // 2), dma(S // 2),
            dma(2 * M), dma(2 * M), dma(2 * M), dma(2 * M), dma(M), dma(M), dma(4), dma(4),
            dma(2 * nz), dma(2 * nz),
        ],
        compiler_params=pltpu.CompilerParams(
            collective_id=0, has_side_effects=True, vmem_limit_bytes=60 * 1024 * 1024
        ),
    )(
        starts[0], holes, rate, zones.reshape(2 * nz, nx),
        htc, gas, hold, duration, inv_x, inv_y, inv_z,
    )
    return (steps.astype(F32) * unit)[None]


def solution(mesh):
    return jax.shard_map(
        functools.partial(per_device, mesh.shape["tm"], mesh.shape["space"]),
        mesh=mesh,
        in_specs=(
            P("tm", "space", None, None),
            P("space", None, None),
            P("space", None, None),
            P(None, "space", None),
            P(),
            P("tm", None),
            P("tm"),
            P("tm"),
            P(),
            P(),
            P(),
        ),
        out_specs=P("tm", "space", None, None),
        check_vma=False,
    )
```

time: 103 us -> 87.4 us (0.85)
  the two profiles are of different devices: /device:TPU:70 before, /device:TPU:2 now
where the time goes in v3:
time: 87.4 us; the launch traced here: 87.3 us
  Pallas kernels  83.8 us (96%)
  other arithmetic  2.19 us (3%)
  between operations  1.3 us (1%)
    pallas_call x1, Pallas kernels, per_device(): pl.pallas_call(functools.partial(kernel, T, S), out_shape=(jax.ShapeDtype...  83.8 us
    broadcast_in_dim x1, other arithmetic, per_device(): return (steps.astype(F32) * unit)[None]  2.19 us

profile of v3, /device:TPU:2, one launch (start us, length us, event | category | flops | bytes accessed | tf_op | source)
XLA Modules:
  0.0 87.3 jit_solution(4772523392473017106)
XLA Ops:
  1.3 83.8 %shard_map.109 = (s16[16,128,128]{2,1,0:T(8,128)(2,1)}, f32[16,1,128]{2,1,0:T(1,128)}) custom-call(f32[16,128,128]{2,1,0:T(8,128)} %bitcast.5, s32[16,128,128]{2,1,0:T(8,128)} %holes_in.1, f32[16,128,128]{2,1,0:T(8,128)} %rate_in.1, s32[32,128]{1,0:T(8,128)} %bitcast.6, f32[8]{0:T(128)} %htc.1, f32[1,8]{1,0:T(1,128)} %gas.1, f32[1]{0:T(128)S(6)} %copy.12.hold, ...), custom_call_target="tpu_custom_call" | custom-call | tf_op jit(solution)/shard_map/pallas_call | solution.py:461
  85.1 2.2 %multiply_bitcast_fusion = f32[1,16,128,128]{3,2,1,0:T(8,128)} fusion(s16[16,128,128]{2,1,0:T(8,128)(2,1)} %get-tuple-element.7, f32[16,128]{1,0:T(8,128)} %bitcast.7), kind=kLoop, calls=%fused_computation | loop fusion | flops 524288 | bytes 1581056 | tf_op jit(solution)/shard_map/broadcast_in_dim | solution.py:498

commit v4 on v3

--- a/solution.py
+++ b/solution.py
@@ -19,13 +19,18 @@
     lax.fori_loop(0, count, lambda i, c: (body(i), c)[1], 0)
 
 
+def grouped(count, body):
+    width = next(w for w in (4, 3, 2, 1) if count % w == 0)
+    loop(count // width, lambda g: body([g * width + i for i in range(width)]))
+
+
 def kernel(
     T, S,
     u_in, holes_in, rate_in, zones_in, htc, gas, hold, duration, inv_x_in, inv_y_in, inv_z_in,
     out_q, out_u,
     u, holes, rate, zones, inv_x, inv_y, inv_z, load_s,
     va, vb, q, iyt, rows_tab, coef_tab, temp_tab, meta, meta_pt,
-    planar, turned, cs, cr, es, aff, px, ver, ps, jm, gf,
+    planar, turned, cs, cr, es, aff, px, ver, ps, jm, gf, states,
     eq, eu, er_q, er_u, gs_q, gs_u, gr_q, gr_u, is_q, is_u, ir_q, ir_u, oq, ou,
     halo_s, halo_r, meta_s, meta_r, c_s, c_r, e_s, e_r, swap_s, swap_r,
     g_s, g_r, i_s, i_r, give_s, give_r, hb_s, hb_r, o_s, o_r,
@@ -183,12 +188,14 @@
         block = turned[pl.ds(to * blk, blk), :]
         return block.reshape(xb, nz, ny).astype(BF16)
 
-    def c_send(k):
-        to = lax.rem(s + 1 + k, S)
-        cs[pl.ds(to * xb, xb)] = c_block(to)
-        c_copy(k).start()
-
-    loop(S - 1, c_send)
+    def c_send(ks):
+        tos = [lax.rem(s + 1 + k, S) for k in ks]
+        for to in tos:
+            cs[pl.ds(to * xb, xb)] = c_block(to)
+        for k in ks:
+            c_copy(k).start()
+
+    grouped(S - 1, c_send)
     cr[s] = c_block(s)
 
     def decay(m, speed):
@@ -199,7 +206,9 @@
 
     def base(k):
         field = lines(u, k)
-        aff[k] = field - decay(meta, lines(rate, k)) * field
+        rest = field - decay(meta, lines(rate, k)) * field
+        for r in range(ratio):
+            aff[k, r] = rest[r * rb : r * rb + rb]
 
     loop(S, base)
     mates.wait_recv()
@@ -216,27 +225,40 @@
             inv_z[...], cr[:, x].reshape(S * nz, ny), preferred_element_type=F32
         )
 
-    def solution_of(k):
-        return es[pl.ds(pl.multiple_of(k * blk, blk), blk), :]
-
-    def e_copies(to):
+    def e_copies(to, r):
+        i, j = to * ratio + r, s * ratio + r
         return (
-            remote(eq.at[to], er_q.at[s], e_s.at[to], e_r.at[s], t, to),
-            remote(eu.at[to], er_u.at[s], e_s.at[S + to], e_r.at[S + s], t, to),
-        )
-
-    def e_send(k):
-        to = lax.rem(s + 1 + k, S)
-        eq[to], eu[to] = coded(solution_of(to))
-        for c in e_copies(to):
+            remote(eq.at[to, r], er_q.at[s, r], e_s.at[i], e_r.at[j], t, to),
+            remote(
+                eu.at[to, r], er_u.at[s, r], e_s.at[S * ratio + i], e_r.at[S * ratio + j], t, to
+            ),
+        )
+
+    def start(copies):
+        for c in copies:
             c.start()
 
-    loop(S - 1, e_send)
-
-    def swap(k):
+    def e_send(r):
+        def body(ks):
+            tos = [lax.rem(s + 1 + k, S) for k in ks]
+            codes = [
+                coded(es[pl.ds(pl.multiple_of(to * blk + r * rb, rb), rb), :]) for to in tos
+            ]
+            for to, (steps, unit) in zip(tos, codes):
+                eq[to, r], eu[to, r] = steps, unit
+            for to in tos:
+                pl.when(to != s)(lambda to=to: start(e_copies(to, r)))
+
+        grouped(S, body)
+        er_q[s, r], er_u[s, r] = eq[s, r], eu[s, r]
+
+    for r in range(ratio):
+        e_send(r)
+
+    def swap(j, r):
+        i = j * ratio + r
         return remote(
-            aff.at[k], px.at[lax.rem(k, H)],
-            swap_s.at[lax.rem(k, H)], swap_r.at[lax.rem(k, H)], mate, s,
+            aff.at[(1 - core) * H + j, r], px.at[j, r], swap_s.at[i], swap_r.at[i], mate, s
         )
 
     def g_copies(to):
@@ -246,70 +268,66 @@
             remote(gs_u.at[to], gr_u.at[chip], g_s.at[M + to], g_r.at[M + chip], there, s),
         )
 
-    def maps(k, rows):
-        own, other = aff[k, rows, :], px[lax.rem(k, H), rows, :]
+    def maps(j, r):
+        own, other = aff[core * H + j, r], px[j, r]
         return jnp.where(core == 0, own, other), jnp.where(core == 0, other, own)
 
-    def take(frm, part):
-        ver[frm] = part
-        aff[frm] = aff[frm] + part
-
-        @pl.when(frm // H != core)
-        def _():
-            swap(frm).start()
-
-    def e_take(k):
-        frm = lax.rem(s + S - 1 - k, S)
-        remote(eq.at[0], er_q.at[frm], e_s.at[frm], e_r.at[frm], t, frm).wait_recv()
-        remote(eu.at[0], er_u.at[frm], e_s.at[frm], e_r.at[S + frm], t, frm).wait_recv()
-        take(frm, decoded(er_q[frm], er_u[frm]))
-
-    def composed(k):
-        frm = lax.rem(s + S - k, S)
-
-        @pl.when(frm // H == core)
-        def _():
-            swap(frm).wait_recv()
-            speed = lines(rate, frm)
-            for r in range(ratio):
-                block = lax.rem(frm, H) * ratio + r
-                lo, hi = maps(frm, slice(r * rb, r * rb + rb))
-                steps, unit = coded(decay(high, speed[r * rb : r * rb + rb]) * lo + hi)
-                gs_q[block] = steps
-                gs_u[block] = jnp.concatenate(
-                    [low[0:1] * high[0:1], low[1:2] + high[1:2], unit, unit], axis=0
-                )
-
-                @pl.when(block != chip)
+    def e_take(r):
+        def body(ks):
+            frms = [lax.rem(s + S - k, S) for k in ks]
+            for frm in frms:
+
+                @pl.when(frm != s)
                 def _():
-                    for c in g_copies(block):
-                        c.start()
-
-    take(s, solution_of(s))
-    e_take(0)
-
-    def stream(k):
-        e_take(k + 1)
-        composed(k)
-
-    loop(S - 2, stream)
-    composed(S - 2)
-    composed(S - 1)
-    gr_q[chip] = gs_q[chip]
-    gr_u[chip] = gs_u[chip]
-
-    def plane(ref, z):
-        return ref[:, pl.ds(pl.multiple_of(z * xb, xb), xb), :]
-
-    def defect(z):
-        rows = pl.ds(pl.multiple_of(z * xb, xb), xb)
-        ver[:, rows, :] = ver[:, rows, :] - planar[z].reshape(S, xb, ny)
-
-    loop(nz, defect)
+                    i = frm * ratio + r
+                    remote(
+                        eq.at[0, r], er_q.at[frm, r], e_s.at[i], e_r.at[i], t, frm
+                    ).wait_recv()
+                    remote(
+                        eu.at[0, r], er_u.at[frm, r], e_s.at[i], e_r.at[S * ratio + i], t, frm
+                    ).wait_recv()
+
+            parts = [decoded(er_q[frm, r], er_u[frm, r]) for frm in frms]
+            sums = [aff[frm, r] + part for frm, part in zip(frms, parts)]
+            for frm, part, total in zip(frms, parts, sums):
+                ver[frm, r] = part
+                aff[frm, r] = total
+            for frm in frms:
+                pl.when(frm // H != core)(lambda frm=frm: swap(lax.rem(frm, H), r).start())
+
+        grouped(S, body)
 
     def cells(ref, block):
         k, r = core * H + block // ratio, lax.rem(block, ratio)
         return ref.at[pl.ds(r * zr, zr), pl.ds(pl.multiple_of(k * xb, xb), xb)]
+
+    def compose(r):
+        loop(H, lambda j: swap(j, r).wait_recv())
+
+        def body(js):
+            js = [lax.rem(chip // ratio + 1 + j, H) for j in js]
+            codes = []
+            for j in js:
+                lo, hi = maps(j, r)
+                speed = cells(rate, j * ratio + r)[...].reshape(rb, ny)
+                codes.append(coded(decay(high, speed) * lo + hi))
+            for j, (steps, unit) in zip(js, codes):
+                gs_q[j * ratio + r] = steps
+                gs_u[j * ratio + r] = jnp.concatenate(
+                    [low[0:1] * high[0:1], low[1:2] + high[1:2], unit, unit], axis=0
+                )
+            for j in js:
+                block = j * ratio + r
+                pl.when(block != chip)(lambda block=block: start(g_copies(block)))
+
+        grouped(H, body)
+
+    def defect(r):
+        def body(z):
+            rows = pl.ds(pl.multiple_of(z * xb, xb), xb)
+            ver[:, r, rows, :] = ver[:, r, rows, :] - planar[r * zr + z].reshape(S, xb, ny)
+
+        loop(zr, body)
 
     def i_copies(to):
         there = 2 * to + core
@@ -318,40 +336,62 @@
             remote(is_u.at[to], ir_u.at[chip], i_s.at[M + to], i_r.at[M + chip], there, s),
         )
 
-    speed = cells(rate, chip)[...].reshape(rb, ny)
-
-    def close(m, carry):
-        total, kept, length = carry
-
-        @pl.when(m != chip)
-        def _():
-            there = 2 * m + core
-            remote(gs_q.at[0], gr_q.at[m], g_s.at[m], g_r.at[m], there, s).wait_recv()
-            remote(gs_u.at[0], gr_u.at[m], g_s.at[m], g_r.at[M + m], there, s).wait_recv()
-
-        h, d = gr_u[m, 0:1], gr_u[m, 1:2]
-        factor = h * jnp.exp(-(speed * d))
-        term = decoded(gr_q[m], gr_u[m, 2:3])
-        jm[m] = factor
-        gf[m] = term
-        return factor * total + term, kept * h, length + d
-
-    total, kept, length = lax.fori_loop(
-        0, M, close,
-        (jnp.zeros((rb, ny), F32), jnp.ones((1, ny), F32), jnp.zeros((1, ny), F32)),
-    )
-
-    def march(m, state):
-        is_q[m], is_u[m] = coded(state)
-
-        @pl.when(m != chip)
-        def _():
-            for c in i_copies(m):
-                c.start()
-
-        return jm[m] * state + gf[m]
-
-    lax.fori_loop(0, M, march, total / (1.0 - kept * jnp.exp(-(speed * length))))
+    def scan():
+        gr_q[chip] = gs_q[chip]
+        gr_u[chip] = gs_u[chip]
+        speed = cells(rate, chip)[...].reshape(rb, ny)
+
+        def arrive(ks):
+            ms = [lax.rem(chip + k, M) for k in ks]
+            for m in ms:
+
+                @pl.when(m != chip)
+                def _():
+                    there = 2 * m + core
+                    remote(gs_q.at[0], gr_q.at[m], g_s.at[m], g_r.at[m], there, s).wait_recv()
+                    remote(
+                        gs_u.at[0], gr_u.at[m], g_s.at[m], g_r.at[M + m], there, s
+                    ).wait_recv()
+
+            pairs = [
+                (
+                    gr_u[m, 0:1] * jnp.exp(-(speed * gr_u[m, 1:2])),
+                    decoded(gr_q[m], gr_u[m, 2:3]),
+                )
+                for m in ms
+            ]
+            for m, (factor, term) in zip(ms, pairs):
+                jm[m], gf[m] = factor, term
+
+        grouped(M, arrive)
+        total = gf[0]
+        kept, length = gr_u[0, 0:1], gr_u[0, 1:2]
+        for m in range(1, M):
+            total = jm[m] * total + gf[m]
+            kept, length = kept * gr_u[m, 0:1], length + gr_u[m, 1:2]
+        state = total / (1.0 - kept * jnp.exp(-(speed * length)))
+        for m in range(M):
+            following = jm[m] * state + gf[m]
+            states[m] = state
+            state = following
+
+        def leave(ks):
+            ms = [lax.rem(chip + 1 + k, M) for k in ks]
+            codes = [coded(states[m]) for m in ms]
+            for m, (steps, unit) in zip(ms, codes):
+                is_q[m], is_u[m] = steps, unit
+            for m in ms:
+                pl.when(m != chip)(lambda m=m: start(i_copies(m)))
+
+        grouped(M, leave)
+        ir_q[chip] = is_q[chip]
+        ir_u[chip] = is_u[chip]
+
+    for r in range(ratio):
+        e_take(r)
+        compose(r)
+        defect(r)
+        pl.when(lax.rem(chip, ratio) == r)(scan)
 
     def give(block):
         return remote(
@@ -359,52 +399,66 @@
             give_s.at[block], give_r.at[block], mate, s,
         )
 
-    def predict(block, p0):
-        k, r = core * H + block // ratio, lax.rem(block, ratio)
-        lo, _ = maps(k, pl.ds(pl.multiple_of(r * rb, rb), rb))
-        p1 = decay(low, cells(rate, block)[...].reshape(rb, ny)) * p0 + lo
-        mine = jnp.where(core == 0, p0, p1).reshape(zr, xb, ny)
-        there = (pl.ds(r * zr, zr), pl.ds(pl.multiple_of(k * xb, xb), xb))
-        here = (pl.ds(1 + r * zr, zr), pl.ds(pl.multiple_of(k * xb, xb), xb))
-        vb[here] = mine
-        q[here] = conductivity(mine)
-        ps[there] = jnp.where(core == 0, p1, p0).reshape(zr, xb, ny)
-        give(block).start()
-
-    predict(chip, decoded(is_q[chip], is_u[chip]))
-
-    def i_take(k):
-        frm = lax.rem(chip + 1 + k, M)
-        there = 2 * frm + core
-        remote(is_q.at[0], ir_q.at[frm], i_s.at[frm], i_r.at[frm], there, s).wait_recv()
-        remote(is_u.at[0], ir_u.at[frm], i_s.at[frm], i_r.at[M + frm], there, s).wait_recv()
-        predict(frm, decoded(ir_q[frm], ir_u[frm]))
-
-    loop(M - 1, i_take)
+    def i_take(r):
+        def body(js):
+            js = [lax.rem(chip // ratio + j, H) for j in js]
+            blocks = [j * ratio + r for j in js]
+            for frm in blocks:
+
+                @pl.when(frm != chip)
+                def _():
+                    there = 2 * frm + core
+                    remote(
+                        is_q.at[0], ir_q.at[frm], i_s.at[frm], i_r.at[frm], there, s
+                    ).wait_recv()
+                    remote(
+                        is_u.at[0], ir_u.at[frm], i_s.at[frm], i_r.at[M + frm], there, s
+                    ).wait_recv()
+
+            fields = []
+            for j, block in zip(js, blocks):
+                lo, _ = maps(j, r)
+                p0 = decoded(ir_q[block], ir_u[block])
+                p1 = decay(low, cells(rate, block)[...].reshape(rb, ny)) * p0 + lo
+                mine = jnp.where(core == 0, p0, p1).reshape(zr, xb, ny)
+                theirs = jnp.where(core == 0, p1, p0).reshape(zr, xb, ny)
+                fields.append((mine, theirs, conductivity(mine)))
+            for block, (mine, theirs, cond) in zip(blocks, fields):
+                cells(ps, block)[...] = theirs
+                cells(vb.at[pl.ds(1, nz)], block)[...] = mine
+                cells(q.at[pl.ds(1, nz)], block)[...] = cond
+            for block in blocks:
+                give(block).start()
+
+        grouped(H, body)
+
     xs = pl.ds(pl.multiple_of(base_x, nx // 2), nx // 2)
-    hb = []
-    for i, (src, z, side, to) in enumerate(
-        (
-            (ps, 0, 1, down), (ps, nz - 1, 0, up), (vb, 1, 1, down), (vb, nz, 0, up),
-        )
-    ):
-        hb.append(
-            remote(
-                src.at[z, xs], vb.at[side * (nz + 1), xs],
-                hb_s.at[i], hb_r.at[2 * side + core], mate if i < 2 else t, to,
-            )
-        )
-    for c in hb:
-        c.start()
-
-    def give_take(k):
-        frm = lax.rem(chip + k, M)
-        x = (1 - core) * H + frm // ratio
-        where = (pl.ds(1 + lax.rem(frm, ratio) * zr, zr), pl.ds(pl.multiple_of(x * xb, xb), xb))
-        remote(cells(ps, frm), vb.at[where], give_s.at[frm], give_r.at[frm], mate, s).wait_recv()
-        q[where] = conductivity(vb[where])
-
-    loop(M, give_take)
+    hb = [
+        remote(
+            src.at[z, xs], vb.at[side * (nz + 1), xs],
+            hb_s.at[i], hb_r.at[2 * side + core], mate if i % 2 == 0 else t, to,
+        )
+        for i, (src, z, side, to) in enumerate(
+            ((ps, 0, 1, down), (vb, 1, 1, down), (ps, nz - 1, 0, up), (vb, nz, 0, up))
+        )
+    ]
+
+    def give_take(r):
+        def body(js):
+            js = [lax.rem(chip // ratio + j, H) for j in js]
+            places = []
+            for j in js:
+                block, x = j * ratio + r, (1 - core) * H + j
+                where = (pl.ds(1 + r * zr, zr), pl.ds(pl.multiple_of(x * xb, xb), xb))
+                remote(
+                    cells(ps, block), vb.at[where], give_s.at[block], give_r.at[block], mate, s
+                ).wait_recv()
+                places.append(where)
+            conds = [conductivity(vb[where]) for where in places]
+            for where, cond in zip(places, conds):
+                q[where] = cond
+
+        grouped(H, body)
 
     def o_copies(z):
         return (
@@ -412,15 +466,30 @@
             remote(ou.at[z], out_u.at[z], o_s.at[nz + z], o_r.at[nz + z], nt, s),
         )
 
+    def plane(z):
+        rows = pl.ds(pl.multiple_of(lax.rem(z, zr) * xb, xb), xb)
+        return ver[:, z // zr, rows, :].reshape(nx, ny)
+
     def second(z0, z1):
         c0, p = solved(vb, z0)
         c1, r = solved(vb, z1)
-        oq[z0], ou[z0] = coded(c0 + p + plane(ver, z0).reshape(nx, ny))
-        oq[z1], ou[z1] = coded(c1 + r + plane(ver, z1).reshape(nx, ny))
+        first_code = coded(c0 + p + plane(z0))
+        second_code = coded(c1 + r + plane(z1))
+        oq[z0], ou[z0] = first_code
+        oq[z1], ou[z1] = second_code
         for c in o_copies(z0) + o_copies(z1):
             c.start()
 
-    loop((nz - 2) // 2, lambda i: second(1 + 2 * i, 2 + 2 * i))
+    for r in range(ratio):
+        i_take(r)
+        if r == 0:
+            start(hb[:2])
+        if r == ratio - 1:
+            start(hb[2:])
+        give_take(r)
+        z0 = max(1, r * zr - 1)
+        pairs = ((r + 1) * zr - 1 - z0) // 2
+        loop(pairs, lambda i, z0=z0: second(z0 + 2 * i, z0 + 1 + 2 * i))
     for side in range(2):
         for c in range(2):
             remote(
@@ -436,8 +505,9 @@
 
     sent(halo + [mates] + hb)
     loop(S - 1, lambda k: c_copy(k).wait_send())
-    loop(S - 1, lambda k: sent(e_copies(lax.rem(s + 1 + k, S))))
-    loop(H, lambda k: swap((1 - core) * H + k).wait_send())
+    for r in range(ratio):
+        loop(S - 1, lambda k, r=r: sent(e_copies(lax.rem(s + 1 + k, S), r)))
+        loop(H, lambda j, r=r: swap(j, r).wait_send())
     loop(M - 1, lambda k: sent(g_copies(lax.rem(chip + 1 + k, M))))
     loop(M - 1, lambda k: sent(i_copies(lax.rem(chip + 1 + k, M))))
     loop(M, lambda k: give(k).wait_send())
@@ -453,6 +523,7 @@
     _, nz, nx, ny = starts.shape
     xb, M = nx // S, T // 2
     blk, rb = nz * xb, nz * nx // 2 // M
+    ratio = blk // rb
     hbm = pl.BlockSpec(memory_space=pltpu.HBM)
     smem = pl.BlockSpec(memory_space=pltpu.SMEM)
     dma = lambda n: pltpu.SemaphoreType.DMA((n,))
@@ -476,15 +547,16 @@
             v32(8, ny), v32(8, ny),
             v32(nz, nx, ny), v32(nx * nz, ny),
             pltpu.VMEM((nx, nz, ny), BF16), pltpu.VMEM((S, xb, nz, ny), BF16),
-            v32(S * blk, ny), v32(S, blk, ny), v32(S // 2, blk, ny),
-            v32(S, blk, ny), v32(nz, nx, ny),
-            v32(M, rb, ny), v32(M, rb, ny),
-            i16(S, blk, ny), v32(S, 1, ny), i16(S, blk, ny), v32(S, 1, ny),
+            v32(S * blk, ny), v32(S, ratio, rb, ny), v32(S // 2, ratio, rb, ny),
+            v32(S, ratio, rb, ny), v32(nz, nx, ny),
+            v32(M, rb, ny), v32(M, rb, ny), v32(M, rb, ny),
+            i16(S, ratio, rb, ny), v32(S, ratio, 1, ny),
+            i16(S, ratio, rb, ny), v32(S, ratio, 1, ny),
             i16(M, rb, ny), v32(M, 4, ny), i16(M, rb, ny), v32(M, 4, ny),
             i16(M, rb, ny), v32(M, 1, ny), i16(M, rb, ny), v32(M, 1, ny),
             i16(nz, nx, ny), v32(nz, 1, ny),
-            dma(2), dma(2), dma(1), dma(1), dma(S), dma(S), dma(2 * S), dma(2 * S),
-            dma(S // 2), dma(S // 2),
+            dma(2), dma(2), dma(1), dma(1), dma(S), dma(S),
+            dma(2 * S * ratio), dma(2 * S * ratio), dma(M), dma(M),
             dma(2 * M), dma(2 * M), dma(2 * M), dma(2 * M), dma(M), dma(M), dma(4), dma(4),
             dma(2 * nz), dma(2 * nz),
         ],

time: 87.4 us -> 91.8 us (1.050)
  Pallas kernels: 83.8 us -> 88.1 us
    pallas_call x1, Pallas kernels: 83.8 us -> 88.1 us  [per_device(): pl.pallas_call(functools.partial(kernel, T, S), out_shape=(jax.ShapeDtype...]
where the time goes in v4:
time: 91.8 us; the launch traced here: 91.6 us
  Pallas kernels  88.1 us (96%)
  other arithmetic  2.19 us (2%)
  between operations  1.3 us (1%)
    pallas_call x1, Pallas kernels, per_device(): pl.pallas_call(functools.partial(kernel, T, S), out_shape=(jax.ShapeDtype...  88.1 us
    broadcast_in_dim x1, other arithmetic, per_device(): return (steps.astype(F32) * unit)[None]  2.19 us

profile of v4, /device:TPU:2, one launch (start us, length us, event | category | flops | bytes accessed | tf_op | source)
XLA Modules:
  0.0 91.6 jit_solution(8256538591850746920)
XLA Ops:
  1.3 88.1 %shard_map.109 = (s16[16,128,128]{2,1,0:T(8,128)(2,1)}, f32[16,1,128]{2,1,0:T(1,128)}) custom-call(f32[16,128,128]{2,1,0:T(8,128)} %bitcast.5, s32[16,128,128]{2,1,0:T(8,128)} %holes_in.1, f32[16,128,128]{2,1,0:T(8,128)} %rate_in.1, s32[32,128]{1,0:T(8,128)} %bitcast.6, f32[8]{0:T(128)} %htc.1, f32[1,8]{1,0:T(1,128)} %gas.1, f32[1]{0:T(128)S(6)} %copy.12.hold, ...), custom_call_target="tpu_custom_call" | custom-call | tf_op jit(solution)/shard_map/pallas_call | solution.py:532
  89.4 2.2 %multiply_bitcast_fusion = f32[1,16,128,128]{3,2,1,0:T(8,128)} fusion(s16[16,128,128]{2,1,0:T(8,128)(2,1)} %get-tuple-element.7, f32[16,128]{1,0:T(8,128)} %bitcast.7), kind=kLoop, calls=%fused_computation | loop fusion | flops 524288 | bytes 1581056 | tf_op jit(solution)/shard_map/broadcast_in_dim | solution.py:570

commit v5 on v3

--- a/solution.py
+++ b/solution.py
@@ -25,7 +25,7 @@
     out_q, out_u,
     u, holes, rate, zones, inv_x, inv_y, inv_z, load_s,
     va, vb, q, iyt, rows_tab, coef_tab, temp_tab, meta, meta_pt,
-    planar, turned, cs, cr, es, aff, px, ver, ps, jm, gf,
+    planar, turned, cs, cr, es, aff, px, ver, ps, jm, gf, states,
     eq, eu, er_q, er_u, gs_q, gs_u, gr_q, gr_u, is_q, is_u, ir_q, ir_u, oq, ou,
     halo_s, halo_r, meta_s, meta_r, c_s, c_r, e_s, e_r, swap_s, swap_r,
     g_s, g_r, i_s, i_r, give_s, give_r, hb_s, hb_r, o_s, o_r,
@@ -158,23 +158,36 @@
         planar[z] = p
         turned[pl.ds(z, nx, stride=nz), :] = p
 
+    def pair(i):
+        return 1 + 2 * i, lax.rem(2 + 2 * i, nz)
+
     def first(i):
-        z = 1 + 2 * i
-        _, p = solved(va, z)
-        _, r = solved(va, z + 1)
-        keep(z, p)
-        keep(z + 1, r)
-
-    loop((nz - 2) // 2, first)
-    halo[0].wait_recv()
-    halo[1].wait_recv()
-    edges(va)
-    p, r = solved(va, 0)[1], solved(va, nz - 1)[1]
-    keep(0, p)
-    keep(nz - 1, r)
+        @pl.when(i == nz // 2 - 1)
+        def _():
+            halo[0].wait_recv()
+            halo[1].wait_recv()
+            edges(va)
+
+        z0, z1 = pair(i)
+        _, p = solved(va, z0)
+        _, r = solved(va, z1)
+        keep(z0, p)
+        keep(z1, r)
+
+    loop(nz // 2, first)
+
+    def stride(k, size=S):
+        odd = lax.rem(k, 2)
+        return (1 - odd) * (1 + k // 2) + odd * (size - 1 - k // 2)
+
+    def to_of(k):
+        return lax.rem(s + stride(k), S)
+
+    def from_of(k):
+        return lax.rem(s + S - stride(k), S)
 
     def c_copy(k):
-        to = lax.rem(s + 1 + k, S)
+        to = to_of(k)
         return remote(
             cs.at[pl.ds(to * xb, xb)], cr.at[s], c_s.at[to], c_r.at[s], t, to
         )
@@ -184,7 +197,7 @@
         return block.reshape(xb, nz, ny).astype(BF16)
 
     def c_send(k):
-        to = lax.rem(s + 1 + k, S)
+        to = to_of(k)
         cs[pl.ds(to * xb, xb)] = c_block(to)
         c_copy(k).start()
 
@@ -211,10 +224,12 @@
         remote(cs.at[pl.ds(0, xb)], cr.at[frm], c_s.at[frm], c_r.at[frm], t, frm).wait_recv()
 
     loop(S - 1, c_wait)
-    for x in range(xb):
+    def solve(x):
         es[pl.ds(x, S * nz, stride=xb), :] = jnp.dot(
             inv_z[...], cr[:, x].reshape(S * nz, ny), preferred_element_type=F32
         )
+
+    loop(xb, solve)
 
     def solution_of(k):
         return es[pl.ds(pl.multiple_of(k * blk, blk), blk), :]
@@ -226,7 +241,7 @@
         )
 
     def e_send(k):
-        to = lax.rem(s + 1 + k, S)
+        to = to_of(k)
         eq[to], eu[to] = coded(solution_of(to))
         for c in e_copies(to):
             c.start()
@@ -259,14 +274,12 @@
             swap(frm).start()
 
     def e_take(k):
-        frm = lax.rem(s + S - 1 - k, S)
+        frm = from_of(k)
         remote(eq.at[0], er_q.at[frm], e_s.at[frm], e_r.at[frm], t, frm).wait_recv()
         remote(eu.at[0], er_u.at[frm], e_s.at[frm], e_r.at[S + frm], t, frm).wait_recv()
         take(frm, decoded(er_q[frm], er_u[frm]))
 
-    def composed(k):
-        frm = lax.rem(s + S - k, S)
-
+    def composed(frm):
         @pl.when(frm // H == core)
         def _():
             swap(frm).wait_recv()
@@ -288,13 +301,14 @@
     take(s, solution_of(s))
     e_take(0)
 
+    composed(s)
+
     def stream(k):
         e_take(k + 1)
-        composed(k)
+        composed(from_of(k))
 
     loop(S - 2, stream)
-    composed(S - 2)
-    composed(S - 1)
+    composed(from_of(S - 2))
     gr_q[chip] = gs_q[chip]
     gr_u[chip] = gs_u[chip]
 
@@ -342,16 +356,18 @@
     )
 
     def march(m, state):
-        is_q[m], is_u[m] = coded(state)
-
-        @pl.when(m != chip)
-        def _():
-            for c in i_copies(m):
-                c.start()
-
+        states[m] = state
         return jm[m] * state + gf[m]
 
     lax.fori_loop(0, M, march, total / (1.0 - kept * jnp.exp(-(speed * length))))
+
+    def leave(k):
+        to = lax.rem(chip + stride(k, M), M)
+        is_q[to], is_u[to] = coded(states[to])
+        for c in i_copies(to):
+            c.start()
+
+    loop(M - 1, leave)
 
     def give(block):
         return remote(
@@ -371,10 +387,10 @@
         ps[there] = jnp.where(core == 0, p1, p0).reshape(zr, xb, ny)
         give(block).start()
 
-    predict(chip, decoded(is_q[chip], is_u[chip]))
+    predict(chip, states[chip])
 
     def i_take(k):
-        frm = lax.rem(chip + 1 + k, M)
+        frm = lax.rem(chip + M - stride(k, M), M)
         there = 2 * frm + core
         remote(is_q.at[0], ir_q.at[frm], i_s.at[frm], i_r.at[frm], there, s).wait_recv()
         remote(is_u.at[0], ir_u.at[frm], i_s.at[frm], i_r.at[M + frm], there, s).wait_recv()
@@ -412,7 +428,18 @@
             remote(ou.at[z], out_u.at[z], o_s.at[nz + z], o_r.at[nz + z], nt, s),
         )
 
-    def second(z0, z1):
+    def second(i):
+        @pl.when(i == nz // 2 - 1)
+        def _():
+            for side in range(2):
+                for c in range(2):
+                    remote(
+                        ps.at[0, xs], vb.at[side * (nz + 1), pl.ds(c * (nx // 2), nx // 2)],
+                        hb_s.at[0], hb_r.at[2 * side + c], t, down,
+                    ).wait_recv()
+            edges(vb)
+
+        z0, z1 = pair(i)
         c0, p = solved(vb, z0)
         c1, r = solved(vb, z1)
         oq[z0], ou[z0] = coded(c0 + p + plane(ver, z0).reshape(nx, ny))
@@ -420,15 +447,7 @@
         for c in o_copies(z0) + o_copies(z1):
             c.start()
 
-    loop((nz - 2) // 2, lambda i: second(1 + 2 * i, 2 + 2 * i))
-    for side in range(2):
-        for c in range(2):
-            remote(
-                ps.at[0, xs], vb.at[side * (nz + 1), pl.ds(c * (nx // 2), nx // 2)],
-                hb_s.at[0], hb_r.at[2 * side + c], t, down,
-            ).wait_recv()
-    edges(vb)
-    second(0, nz - 1)
+    loop(nz // 2, second)
 
     def sent(copies):
         for c in copies:
@@ -478,7 +497,7 @@
             pltpu.VMEM((nx, nz, ny), BF16), pltpu.VMEM((S, xb, nz, ny), BF16),
             v32(S * blk, ny), v32(S, blk, ny), v32(S // 2, blk, ny),
             v32(S, blk, ny), v32(nz, nx, ny),
-            v32(M, rb, ny), v32(M, rb, ny),
+            v32(M, rb, ny), v32(M, rb, ny), v32(M, rb, ny),
             i16(S, blk, ny), v32(S, 1, ny), i16(S, blk, ny), v32(S, 1, ny),
             i16(M, rb, ny), v32(M, 4, ny), i16(M, rb, ny), v32(M, 4, ny),
             i16(M, rb, ny), v32(M, 1, ny), i16(M, rb, ny), v32(M, 1, ny),

time: 87.4 us -> 84.4 us (0.966)
  Pallas kernels: 83.8 us -> 80.7 us
    pallas_call x1, Pallas kernels: 83.8 us -> 80.7 us  [per_device(): pl.pallas_call(functools.partial(kernel, T, S), out_shape=(jax.ShapeDtype...]
where the time goes in v5:
time: 84.4 us; the launch traced here: 84.2 us
  Pallas kernels  80.7 us (96%)
  other arithmetic  2.19 us (3%)
  between operations  1.3 us (2%)
    pallas_call x1, Pallas kernels, per_device(): pl.pallas_call(functools.partial(kernel, T, S), out_shape=(jax.ShapeDtype...  80.7 us
    broadcast_in_dim x1, other arithmetic, per_device(): return (steps.astype(F32) * unit)[None]  2.19 us

profile of v5, /device:TPU:2, one launch (start us, length us, event | category | flops | bytes accessed | tf_op | source)
XLA Modules:
  0.0 84.2 jit_solution(11487670277280471793)
XLA Ops:
  1.3 80.7 %shard_map.109 = (s16[16,128,128]{2,1,0:T(8,128)(2,1)}, f32[16,1,128]{2,1,0:T(1,128)}) custom-call(f32[16,128,128]{2,1,0:T(8,128)} %bitcast.5, s32[16,128,128]{2,1,0:T(8,128)} %holes_in.1, f32[16,128,128]{2,1,0:T(8,128)} %rate_in.1, s32[32,128]{1,0:T(8,128)} %bitcast.6, f32[8]{0:T(128)} %htc.1, f32[1,8]{1,0:T(1,128)} %gas.1, f32[1]{0:T(128)S(6)} %copy.12.hold, ...), custom_call_target="tpu_custom_call" | custom-call | tf_op jit(solution)/shard_map/pallas_call | solution.py:480
  82.0 2.2 %multiply_bitcast_fusion = f32[1,16,128,128]{3,2,1,0:T(8,128)} fusion(s16[16,128,128]{2,1,0:T(8,128)(2,1)} %get-tuple-element.7, f32[16,128]{1,0:T(8,128)} %bitcast.7), kind=kLoop, calls=%fused_computation | loop fusion | flops 524288 | bytes 1581056 | tf_op jit(solution)/shard_map/broadcast_in_dim | solution.py:517

commit v6 on v5

--- a/solution.py
+++ b/solution.py
@@ -25,7 +25,7 @@
     out_q, out_u,
     u, holes, rate, zones, inv_x, inv_y, inv_z, load_s,
     va, vb, q, iyt, rows_tab, coef_tab, temp_tab, meta, meta_pt,
-    planar, turned, cs, cr, es, aff, px, ver, ps, jm, gf, states,
+    planar, turned, cs, cr, es, aff, px, ver, ps, jm, gf, states, still, slope,
     eq, eu, er_q, er_u, gs_q, gs_u, gr_q, gr_u, is_q, is_u, ir_q, ir_u, oq, ou,
     halo_s, halo_r, meta_s, meta_r, c_s, c_r, e_s, e_r, swap_s, swap_r,
     g_s, g_r, i_s, i_r, give_s, give_r, hb_s, hb_r, o_s, o_r,
@@ -118,7 +118,21 @@
         q[0] = conductivity(v[0])
         q[nz + 1] = conductivity(v[nz + 1])
 
-    def solved(v, z):
+    def at_faces(z):
+        turn = lax.rem(ny - 2 * z, ny)
+        on_face = (lane == 0) | (lane == ny - 1)
+        face_coef = jnp.where(on_face, pltpu.roll(coef_tab[...], turn, 1), 0.0)
+        return face_coef, pltpu.roll(temp_tab[...], turn, 1)
+
+    def source_now(z, c):
+        face_coef, face_temp = at_faces(z)
+        cooled = COOLING * holes[z].astype(F32) * (COOLANT - c)
+        return face_coef * (face_temp - c) + cooled
+
+    def source_kept(z, c):
+        return still[z] - slope[z] * c
+
+    def solved(v, z, source):
         c, qc = v[z + 1], q[z + 1]
         outer = (qc + 0.5) * c
         flux = (q[z + 2] + qc) * (v[z + 2] - c) - (q[z] + qc) * (c - v[z])
@@ -128,13 +142,7 @@
             ahead = jnp.where(index == last, -outer, (qn + qc) * (vn - c))
             behind = jnp.where(index == 0, outer, pltpu.roll(ahead, 1, axis))
             flux = flux + ahead - behind
-        turn = lax.rem(ny - 2 * z, ny)
-        face_coef = pltpu.roll(coef_tab[...], turn, 1)
-        face_temp = pltpu.roll(temp_tab[...], turn, 1)
-        on_face = (lane == 0) | (lane == ny - 1)
-        surface = jnp.where(on_face, face_coef * (face_temp - c), 0.0)
-        cooled = COOLING * holes[z].astype(F32) * (COOLANT - c)
-        e = (TIME_STEP * (flux + surface + cooled)).astype(BF16)
+        e = (TIME_STEP * (flux + source(z, c))).astype(BF16)
         x = jnp.dot(inv_x[...], e, preferred_element_type=F32).astype(BF16)
         return c, jnp.dot(x, iyt[...], preferred_element_type=F32)
 
@@ -169,8 +177,8 @@
             edges(va)
 
         z0, z1 = pair(i)
-        _, p = solved(va, z0)
-        _, r = solved(va, z1)
+        _, p = solved(va, z0, source_now)
+        _, r = solved(va, z1, source_now)
         keep(z0, p)
         keep(z1, r)
 
@@ -215,6 +223,14 @@
         aff[k] = field - decay(meta, lines(rate, k)) * field
 
     loop(S, base)
+
+    def keep_source(z):
+        face_coef, face_temp = at_faces(z)
+        hole = COOLING * holes[z].astype(F32)
+        still[z] = face_coef * face_temp + COOLANT * hole
+        slope[z] = face_coef + hole
+
+    loop(nz, keep_source)
     mates.wait_recv()
     low = jnp.where(core == 0, meta[...], meta_pt[...])
     high = jnp.where(core == 0, meta_pt[...], meta[...])
@@ -440,8 +456,8 @@
             edges(vb)
 
         z0, z1 = pair(i)
-        c0, p = solved(vb, z0)
-        c1, r = solved(vb, z1)
+        c0, p = solved(vb, z0, source_kept)
+        c1, r = solved(vb, z1, source_kept)
         oq[z0], ou[z0] = coded(c0 + p + plane(ver, z0).reshape(nx, ny))
         oq[z1], ou[z1] = coded(c1 + r + plane(ver, z1).reshape(nx, ny))
         for c in o_copies(z0) + o_copies(z1):
@@ -498,6 +514,7 @@
             v32(S * blk, ny), v32(S, blk, ny), v32(S // 2, blk, ny),
             v32(S, blk, ny), v32(nz, nx, ny),
             v32(M, rb, ny), v32(M, rb, ny), v32(M, rb, ny),
+            v32(nz, nx, ny), v32(nz, nx, ny),
             i16(S, blk, ny), v32(S, 1, ny), i16(S, blk, ny), v32(S, 1, ny),
             i16(M, rb, ny), v32(M, 4, ny), i16(M, rb, ny), v32(M, 4, ny),
             i16(M, rb, ny), v32(M, 1, ny), i16(M, rb, ny), v32(M, 1, ny),

time: 84.4 us -> 84.5 us (level)
  no operation moved by 1% of the time
where the time goes in v6:
time: 84.5 us; the launch traced here: 84.3 us
  Pallas kernels  80.8 us (96%)
  other arithmetic  2.19 us (3%)
  between operations  1.3 us (2%)
    pallas_call x1, Pallas kernels, per_device(): pl.pallas_call(functools.partial(kernel, T, S), out_shape=(jax.ShapeDtype...  80.8 us
    broadcast_in_dim x1, other arithmetic, per_device(): return (steps.astype(F32) * unit)[None]  2.19 us

profile of v6, /device:TPU:2, one launch (start us, length us, event | category | flops | bytes accessed | tf_op | source)
XLA Modules:
  0.0 84.3 jit_solution(1141223979365537404)
XLA Ops:
  1.3 80.8 %shard_map.109 = (s16[16,128,128]{2,1,0:T(8,128)(2,1)}, f32[16,1,128]{2,1,0:T(1,128)}) custom-call(f32[16,128,128]{2,1,0:T(8,128)} %bitcast.5, s32[16,128,128]{2,1,0:T(8,128)} %holes_in.1, f32[16,128,128]{2,1,0:T(8,128)} %rate_in.1, s32[32,128]{1,0:T(8,128)} %bitcast.6, f32[8]{0:T(128)} %htc.1, f32[1,8]{1,0:T(1,128)} %gas.1, f32[1]{0:T(128)S(6)} %copy.12.hold, ...), custom_call_target="tpu_custom_call" | custom-call | tf_op jit(solution)/shard_map/pallas_call | solution.py:496
  82.2 2.2 %multiply_bitcast_fusion = f32[1,16,128,128]{3,2,1,0:T(8,128)} fusion(s16[16,128,128]{2,1,0:T(8,128)(2,1)} %get-tuple-element.7, f32[16,128]{1,0:T(8,128)} %bitcast.7), kind=kLoop, calls=%fused_computation | loop fusion | flops 524288 | bytes 1581056 | tf_op jit(solution)/shard_map/broadcast_in_dim | solution.py:534
